TPU v7x, 32 devices: a whole 2x2x4 slice. The times are simulated.
32 devices in a mesh: dp: 8 (over z, y), tensor: 4 (over x, core).
Axes of the slice: x: 2, y: 2, z: 4, core: 2. Of those that a mesh axis runs over, the one named last changes fastest.
Arguments:
- images: float32 [32, 197, 768], P('dp'), may hold values from -6 to 6
- counts: int32 [8], P('dp'), may hold values from 3 to 4, as said below
- qkv_weight: bfloat16 [2, 768, 3, 12, 64], P(None, 'dp', None, 'tensor'), may hold values from -0.21875 to 0.21875
- qv_bias: bfloat16 [2, 2, 12, 64], P(None, None, 'tensor', 'dp'), may hold values from -4 to 4
- out_weight: bfloat16 [2, 12, 64, 768], P(None, 'tensor', None, 'dp'), may hold values from -0.625 to 0.625
- up_weight: bfloat16 [2, 768, 3072], P(None, 'dp', 'tensor'), may hold values from -0.21875 to 0.21875
- up_bias: bfloat16 [2, 24, 128], P(None, 'tensor', 'dp'), may hold values from -4 to 4
- down_weight: bfloat16 [2, 3072, 768], P(None, 'tensor', 'dp'), may hold values from -0.109375 to 0.109375
- gains: bfloat16 [2, 2, 768], P(None, None, 'dp'), may hold values from 0.099609375 to 1.8984375
- shifts: bfloat16 [2, 4, 768], P(None, None, 'dp'), may hold values from -4 to 4
- cotangent: float32 [32, 197, 768], P('dp'), may hold values from -6 to 6
Outputs:
- activations: float32 [32, 197, 768], P('dp')
- input_grad: float32 [32, 197, 768], P('dp')
- qkv_grad: float32 [2, 768, 3, 12, 64], P(None, 'dp', None, 'tensor')
- qv_bias_grad: float32 [2, 2, 12, 64], P(None, None, 'tensor', 'dp')
- out_grad: float32 [2, 12, 64, 768], P(None, 'tensor', None, 'dp')
- up_grad: float32 [2, 768, 3072], P(None, 'dp', 'tensor')
- up_bias_grad: float32 [2, 24, 128], P(None, 'tensor', 'dp')
- down_grad: float32 [2, 3072, 768], P(None, 'tensor', 'dp')
- gains_grad: float32 [2, 2, 768], P(None, None, 'dp')
- shifts_grad: float32 [2, 4, 768], P(None, None, 'dp')
Inputs may be any that keep to these rules, and one draw needn't show every extreme that they name: counts[i] is 3 or 4; in every draw some index holds 4 live images and some index holds 3.
All inputs are finite; a program needn't handle non-finite values.
Results may differ from a plain program's by a relative error of at most 0.0003.
Values may be sent and summed in bfloat16 or wider, within the bound.
A program may use at most 192 MiB of HBM per device.

v0:
```python
import math

import jax
import jax.numpy as jnp
from jax import lax
from jax.sharding import PartitionSpec as P

epsilon = 1e-06
highest = lax.Precision.HIGHEST


def product(a, b):
    return jnp.dot(a, b, precision=highest, preferred_element_type=jnp.float32)


def column_sum(values):
    return jnp.sum(values, axis=0)


def norm_keep(values, gain, shift):
    average = jnp.mean(values, axis=-1, keepdims=True)
    centered = values - average
    variance = jnp.mean(centered * centered, axis=-1, keepdims=True)
    inverse = lax.rsqrt(variance + epsilon)
    normed = centered * inverse
    return (normed * gain + shift, normed, inverse)


def norm_back(grad_out, normed, inverse, gain):
    scaled = grad_out * gain
    first_mean = jnp.mean(scaled, axis=-1, keepdims=True)
    second_mean = jnp.mean(scaled * normed, axis=-1, keepdims=True)
    return inverse * (scaled - first_mean - normed * second_mean)


def unpack(gathered):
    qkv_part, bias_part, out_part, up_part, up_bias_part, down_part, gain_part, shift_part = [
        g.astype(jnp.float32) for g in gathered
    ]
    return (
        qkv_part,
        bias_part,
        out_part,
        up_part,
        up_bias_part.reshape(-1),
        down_part,
        gain_part,
        shift_part,
    )


def fetch_forward(params, layer_index):
    qkv_slice, bias_slice, out_slice, up_slice, upb_slice, down_slice, gain_slice, shift_slice = [
        p[layer_index] for p in params
    ]
    return unpack(
        (
            lax.all_gather(qkv_slice, "dp", axis=0, tiled=True),
            lax.all_gather(bias_slice, "dp", axis=2, tiled=True),
            lax.all_gather(out_slice, "dp", axis=2, tiled=True),
            lax.all_gather(up_slice, "dp", axis=0, tiled=True),
            lax.all_gather(upb_slice, "dp", axis=1, tiled=True),
            lax.all_gather(down_slice, "dp", axis=1, tiled=True),
            lax.all_gather(gain_slice, "dp", axis=1, tiled=True),
            lax.all_gather(shift_slice, "dp", axis=1, tiled=True),
        )
    )


def fetch_backward(params, layer_index):
    qkv_slice, bias_slice, out_slice, up_slice, upb_slice, down_slice, gain_slice, shift_slice = [
        p[layer_index] for p in params
    ]
    return unpack(
        (
            lax.all_gather(qkv_slice, "dp", axis=0, tiled=True),
            lax.all_gather(bias_slice, "dp", axis=2, tiled=True),
            lax.all_gather(out_slice, "dp", axis=2, tiled=True),
            lax.all_gather(up_slice, "dp", axis=0, tiled=True),
            lax.all_gather(upb_slice, "dp", axis=1, tiled=True),
            lax.all_gather(down_slice, "dp", axis=1, tiled=True),
            lax.all_gather(gain_slice, "dp", axis=1, tiled=True),
            lax.all_gather(shift_slice, "dp", axis=1, tiled=True),
        )
    )


def gelu_parts(hidden):
    normal_cdf = 0.5 * (1.0 + lax.erf(hidden / math.sqrt(2.0)))
    density = jnp.exp(-0.5 * hidden * hidden) / math.sqrt(2.0 * math.pi)
    return (hidden * normal_cdf, normal_cdf + hidden * density)


def attention_scores(queries, key_rows, factor):
    return jnp.einsum("qhe,khe->hqk", queries, key_rows, precision=highest) * factor


def layer_forward(stream, weights):
    qkv_part, bias_part, out_part, up_part, up_bias_part, down_part, gain_part, shift_part = weights
    model_width, head_count, head_dim = (qkv_part.shape[0], qkv_part.shape[2], qkv_part.shape[3])
    rows = stream.shape[0]
    factor = 1.0 / math.sqrt(head_dim)
    normed_out, normed, inverse = norm_keep(stream, gain_part[0], shift_part[0])
    projected = product(
        normed_out, qkv_part.reshape(model_width, 3 * head_count * head_dim)
    ).reshape(rows, 3, head_count, head_dim)
    queries = projected[:, 0] + bias_part[0]
    key_rows = projected[:, 1]
    values = projected[:, 2] + bias_part[1]
    scores = attention_scores(queries, key_rows, factor)
    row_max = jnp.max(scores, axis=-1, keepdims=True)
    exponent = jnp.exp(scores - row_max)
    row_total = jnp.sum(exponent, axis=-1, keepdims=True)
    log_total = row_max + jnp.log(row_total)
    weights_soft = exponent / row_total
    mixed = jnp.einsum("hqk,khe->qhe", weights_soft, values, precision=highest).reshape(
        rows, head_count * head_dim
    )
    partial_value = product(mixed, out_part.reshape(head_count * head_dim, model_width))
    middle = stream + lax.psum(partial_value, "tensor") + shift_part[2]
    normed_two_out, normed_two, inverse_two = norm_keep(middle, gain_part[1], shift_part[1])
    hidden = product(normed_two_out, up_part) + up_bias_part
    activated, slope = gelu_parts(hidden)
    result = middle + lax.psum(product(activated, down_part), "tensor") + shift_part[3]
    stored = (
        normed,
        inverse,
        normed_out,
        queries,
        key_rows,
        values,
        log_total,
        mixed,
        normed_two,
        inverse_two,
        normed_two_out,
        activated,
        slope,
    )
    return (result, stored)


def layer_backward(grad_out, weights, stored):
    qkv_part, bias_part, out_part, up_part, up_bias_part, down_part, gain_part, shift_part = weights
    (
        normed,
        inverse,
        normed_out,
        queries,
        key_rows,
        values,
        log_total,
        mixed,
        normed_two,
        inverse_two,
        normed_two_out,
        activated,
        slope,
    ) = stored
    model_width, head_count, head_dim = (qkv_part.shape[0], qkv_part.shape[2], qkv_part.shape[3])
    rows = grad_out.shape[0]
    factor = 1.0 / math.sqrt(head_dim)
    shift_three = column_sum(grad_out)
    down_delta = product(activated.T, grad_out)
    grad_hidden = product(grad_out, down_part.T) * slope
    up_delta = product(normed_two_out.T, grad_hidden)
    up_bias_delta = column_sum(grad_hidden)
    grad_norm_two = lax.psum(product(grad_hidden, up_part.T), "tensor")
    gain_one = column_sum(grad_norm_two * normed_two)
    shift_one = column_sum(grad_norm_two)
    grad_middle = grad_out + norm_back(grad_norm_two, normed_two, inverse_two, gain_part[1])
    shift_two = column_sum(grad_middle)
    out_delta = product(mixed.T, grad_middle)
    grad_mixed = product(
        grad_middle, out_part.reshape(head_count * head_dim, model_width).T
    ).reshape(rows, head_count, head_dim)
    weights_soft = jnp.exp(attention_scores(queries, key_rows, factor) - log_total)
    grad_weights = jnp.einsum("qhe,khe->hqk", grad_mixed, values, precision=highest)
    grad_values = jnp.einsum("hqk,qhe->khe", weights_soft, grad_mixed, precision=highest)
    grad_scores = weights_soft * (
        grad_weights - jnp.sum(grad_weights * weights_soft, axis=-1, keepdims=True)
    )
    grad_queries = jnp.einsum("hqk,khe->qhe", grad_scores, key_rows, precision=highest) * factor
    grad_keys = jnp.einsum("hqk,qhe->khe", grad_scores, queries, precision=highest) * factor
    grad_projected = jnp.stack([grad_queries, grad_keys, grad_values], axis=1).reshape(
        rows, 3 * head_count * head_dim
    )
    qkv_delta = product(normed_out.T, grad_projected).reshape(qkv_part.shape)
    bias_delta = jnp.stack([column_sum(grad_queries), column_sum(grad_values)])
    grad_norm_one = lax.psum(
        product(grad_projected, qkv_part.reshape(model_width, 3 * head_count * head_dim).T),
        "tensor",
    )
    gain_zero = column_sum(grad_norm_one * normed)
    shift_zero = column_sum(grad_norm_one)
    grad_in = grad_middle + norm_back(grad_norm_one, normed, inverse, gain_part[0])
    gradient_set = (
        qkv_delta,
        bias_delta,
        out_delta.reshape(out_part.shape),
        up_delta,
        up_bias_delta.reshape(-1, 128),
        down_delta,
        jnp.stack([gain_zero, gain_one]),
        jnp.stack([shift_zero, shift_one, shift_two, shift_three]),
    )
    return (grad_in, gradient_set)


def shards(
    images,
    counts,
    qkv_weight,
    qv_bias,
    out_weight,
    up_weight,
    up_bias,
    down_weight,
    gains,
    shifts,
    cotangent,
):
    params = (qkv_weight, qv_bias, out_weight, up_weight, up_bias, down_weight, gains, shifts)
    slot_count = images.shape[0]
    layer_count = qkv_weight.shape[0]
    present = (jnp.arange(slot_count) < counts[0]).astype(jnp.float32)
    accumulated = [None] * layer_count
    results = []
    grad_images = []
    for image_slot in range(slot_count):
        stream = images[image_slot]
        stored_list = []
        for layer_index in range(layer_count):
            weights = fetch_forward(params, layer_index)
            stream, stored = layer_forward(stream, weights)
            stored_list.append(stored)
        results.append(stream * present[image_slot])
        grad_stream = cotangent[image_slot] * present[image_slot]
        for layer_index in reversed(range(layer_count)):
            weights = fetch_backward(params, layer_index)
            grad_stream, gradient_set = layer_backward(
                grad_stream, weights, stored_list[layer_index]
            )
            if accumulated[layer_index] is None:
                accumulated[layer_index] = gradient_set
            else:
                accumulated[layer_index] = tuple(
                    (a + b for a, b in zip(accumulated[layer_index], gradient_set))
                )
        grad_images.append(grad_stream)
    qkv_total, bias_total, out_total, up_total, upb_total, down_total, gain_total, shift_total = [
        jnp.stack([accumulated[layer_index][member] for layer_index in range(layer_count)])
        for member in range(8)
    ]
    summed = (
        lax.psum_scatter(qkv_total, "dp", scatter_dimension=1, tiled=True),
        lax.psum_scatter(bias_total, "dp", scatter_dimension=3, tiled=True),
        lax.psum_scatter(out_total, "dp", scatter_dimension=3, tiled=True),
        lax.psum_scatter(up_total, "dp", scatter_dimension=1, tiled=True),
        lax.psum_scatter(upb_total, "dp", scatter_dimension=2, tiled=True),
        lax.psum_scatter(down_total, "dp", scatter_dimension=2, tiled=True),
        lax.psum_scatter(gain_total, "dp", scatter_dimension=2, tiled=True),
        lax.psum_scatter(shift_total, "dp", scatter_dimension=2, tiled=True),
    )
    return (
        jnp.stack(results),
        jnp.stack(grad_images),
        summed[0],
        summed[1],
        summed[2],
        summed[3],
        summed[4],
        summed[5],
        summed[6],
        summed[7],
    )


def solution(mesh):
    placed = (
        P("dp", None, None),
        P("dp"),
        P(None, "dp", None, "tensor", None),
        P(None, None, "tensor", "dp"),
        P(None, "tensor", None, "dp"),
        P(None, "dp", "tensor"),
        P(None, "tensor", "dp"),
        P(None, "tensor", "dp"),
        P(None, None, "dp"),
        P(None, None, "dp"),
        P("dp", None, None),
    )
    return jax.shard_map(
        shards,
        mesh=mesh,
        in_specs=placed,
        out_specs=(
            P("dp", None, None),
            P("dp", None, None),
            P(None, "dp", None, "tensor", None),
            P(None, None, "tensor", "dp"),
            P(None, "tensor", None, "dp"),
            P(None, "dp", "tensor"),
            P(None, "tensor", "dp"),
            P(None, "tensor", "dp"),
            P(None, None, "dp"),
            P(None, None, "dp"),
        ),
        check_vma=False,
    )
```

profile of v0, /device:TPU:0, one launch (start us, length us, event | category | flops | bytes accessed | tf_op | source)
XLA Modules:
  0.0 1540.4 jit_solution(14150650223313092346)
XLA Ops:
  10.7 32.2 %all-gather.3 = bf16[1,2,3,64]{2,1,0,3:T(2,128)(2,1)S(1)} all-gather(bf16[1,2,3,8]{2,1,0,3:T(2,128)(2,1)S(1)} %copy.316), channel_id=5, replica_groups=mesh['dp'=8,'tensor'=4] {'dp'}, dimensions={3}, use_global_device_ids=true | all-gather | bytes 864 | tf_op jit(solution)/shard_map/all_gather | solution.py:59
  46.2 31.0 %all-gather = bf16[1,2,768]{1,0,2:T(2,128)(2,1)S(1)} all-gather(bf16[1,2,96]{1,0,2:T(2,128)(2,1)S(1)} %copy.313), channel_id=2, replica_groups=mesh['dp'=8,'tensor'=4] {'dp'}, dimensions={2}, use_global_device_ids=true | all-gather | bytes 3456 | tf_op jit(solution)/shard_map/all_gather | solution.py:64
  77.6 4.6 slice_reduce_fusion.8
  82.2 31.3 %all-gather.1 = bf16[1,4,768]{1,0,2:T(2,128)(2,1)S(1)} all-gather(bf16[1,4,96]{1,0,2:T(2,128)(2,1)S(1)} %copy.314), channel_id=3, replica_groups=mesh['dp'=8,'tensor'=4] {'dp'}, dimensions={2}, use_global_device_ids=true | all-gather | bytes 6912 | tf_op jit(solution)/shard_map/all_gather | solution.py:65
  113.8 10.8 slice_reduce_fusion.6
  124.7 33.8 %all-gather.4 = bf16[1,3,64,768]{2,1,0,3:T(4,128)(2,1)S(1)} all-gather(bf16[1,3,64,96]{2,1,0,3:T(4,128)(2,1)S(1)} %copy.317), channel_id=6, replica_groups=mesh['dp'=8,'tensor'=4] {'dp'}, dimensions={3}, use_global_device_ids=true | all-gather | bytes 331776 | tf_op jit(solution)/shard_map/all_gather | solution.py:60
  159.0 37.9 %all-gather.2 = bf16[1,768,3,3,64]{4,3,2,0,1:T(4,128)(2,1)} all-gather(bf16[1,96,3,3,64]{4,3,2,0,1:T(4,128)(2,1)S(1)} %copy.315), channel_id=4, replica_groups=mesh['dp'=8,'tensor'=4] {'dp'}, dimensions={1}, use_global_device_ids=true | all-gather | bytes 995328 | tf_op jit(solution)/shard_map/all_gather | solution.py:58
  196.9 3.9 copy.185
  200.8 9.1 slice_reduce_fusion.15
  230.6 30.6 %all-gather.11 = bf16[1,2,3,64]{2,1,0,3:T(2,128)(2,1)S(1)} all-gather(bf16[1,2,3,8]{2,1,0,3:T(2,128)(2,1)S(1)} %copy.322), channel_id=13, replica_groups=mesh['dp'=8,'tensor'=4] {'dp'}, dimensions={3}, use_global_device_ids=true | all-gather | bytes 864 | tf_op jit(solution)/shard_map/all_gather | solution.py:59
  261.2 30.7 %all-gather.6 = bf16[1,6,128]{1,0,2:T(2,128)(2,1)S(1)} all-gather(bf16[1,6,16]{1,0,2:T(2,128)(2,1)S(1)} %copy.318), channel_id=8, replica_groups=mesh['dp'=8,'tensor'=4] {'dp'}, dimensions={2}, use_global_device_ids=true | all-gather | bytes 1728 | tf_op jit(solution)/shard_map/all_gather | solution.py:62
  305.0 11.1 all-gather.23.cloned.1.call-done
  316.1 3.7 fusion.30
  328.4 31.2 %all-gather.9 = bf16[1,4,768]{1,0,2:T(2,128)(2,1)S(1)} all-gather(bf16[1,4,96]{1,0,2:T(2,128)(2,1)S(1)} %copy.320), channel_id=11, replica_groups=mesh['dp'=8,'tensor'=4] {'dp'}, dimensions={2}, use_global_device_ids=true | all-gather | bytes 6912 | tf_op jit(solution)/shard_map/all_gather | solution.py:65
  360.7 31.1 %all-gather.8 = bf16[1,2,768]{1,0,2:T(2,128)(2,1)S(1)} all-gather(bf16[1,2,96]{1,0,2:T(2,128)(2,1)S(1)} %copy.319), channel_id=10, replica_groups=mesh['dp'=8,'tensor'=4] {'dp'}, dimensions={2}, use_global_device_ids=true | all-gather | bytes 3456 | tf_op jit(solution)/shard_map/all_gather | solution.py:64
  392.9 34.6 %all-gather.12 = bf16[1,3,64,768]{2,1,0,3:T(4,128)(2,1)} all-gather(bf16[1,3,64,96]{2,1,0,3:T(4,128)(2,1)S(1)} %copy.323), channel_id=14, replica_groups=mesh['dp'=8,'tensor'=4] {'dp'}, dimensions={3}, use_global_device_ids=true | all-gather | bytes 331776 | tf_op jit(solution)/shard_map/all_gather | solution.py:60
  429.0 39.7 %all-gather.10 = bf16[1,768,3,3,64]{4,3,2,0,1:T(4,128)(2,1)} all-gather(bf16[1,96,3,3,64]{4,3,2,0,1:T(4,128)(2,1)} %copy.321), channel_id=12, replica_groups=mesh['dp'=8,'tensor'=4] {'dp'}, dimensions={1}, use_global_device_ids=true | all-gather | bytes 995328 | tf_op jit(solution)/shard_map/all_gather | solution.py:58
  468.7 5.4 copy.197
  474.0 5.7 slice_reduce_fusion.2
  479.8 11.0 slice_reduce_fusion
  515.1 30.6 %all-gather.14 = bf16[1,6,128]{1,0,2:T(2,128)(2,1)S(1)} all-gather(bf16[1,6,16]{1,0,2:T(2,128)(2,1)S(1)} %copy.324), channel_id=16, replica_groups=mesh['dp'=8,'tensor'=4] {'dp'}, dimensions={2}, use_global_device_ids=true | all-gather | bytes 1728 | tf_op jit(solution)/shard_map/all_gather | solution.py:62
  546.4 6.9 fusion.582
  553.3 15.9 %all-reduce.28.cloned.1.call-done = (f32[197,768]{1,0:T(8,128)}, f32[197,768]{1,0:T(8,128)}, f32[197,768]{1,0:T(8,128)}, f32[197,768]{1,0:T(8,128)}) async-done(((f32[197,768]{1,0:T(8,128)}, f32[197,768]{1,0:T(8,128)}, f32[197,768]{1,0:T(8,128)}, f32[197,768]{1,0:T(8,128)}), (f32[197,768]{1,0:T(8,128)}, f32[197,768]{1,0:T(8,128)}, f32[197,768]{1,0:T(8,128)}, ...) | async-done | bytes 2420752 | tf_op jit(solution)/shard_map/psum | solution.py:120
  585.5 12.4 all-gather.27.cloned.1.call-done
  597.9 3.9 fusion.602
  621.2 53.4 %all-reduce.26.cloned.1.call-done = (f32[197,768]{1,0:T(8,128)}, f32[197,768]{1,0:T(8,128)}, f32[197,768]{1,0:T(8,128)}, f32[197,768]{1,0:T(8,128)}) async-done(((f32[197,768]{1,0:T(8,128)}, f32[197,768]{1,0:T(8,128)}, f32[197,768]{1,0:T(8,128)}, f32[197,768]{1,0:T(8,128)}), (f32[197,768]{1,0:T(8,128)}, f32[197,768]{1,0:T(8,128)}, f32[197,768]{1,0:T(8,128)}, ...) | async-done | bytes 2420752 | tf_op jit(solution)/shard_map/psum | solution.py:168
  677.6 3.8 fusion.565
  721.9 49.4 %all-reduce.24.cloned.1.call-done = (f32[197,768]{1,0:T(8,128)}, f32[197,768]{1,0:T(8,128)}, f32[197,768]{1,0:T(8,128)}, f32[197,768]{1,0:T(8,128)}) async-done(((f32[197,768]{1,0:T(8,128)}, f32[197,768]{1,0:T(8,128)}, f32[197,768]{1,0:T(8,128)}, f32[197,768]{1,0:T(8,128)}), (f32[197,768]{1,0:T(8,128)}, f32[197,768]{1,0:T(8,128)}, f32[197,768]{1,0:T(8,128)}, ...) | async-done | bytes 2420752 | tf_op jit(solution)/shard_map/psum | solution.py:190
  801.3 4.3 fusion.150
  805.6 4.3 fusion.159
  810.0 41.4 %all-reduce.22.cloned.1.call-done = (f32[197,768]{1,0:T(8,128)}, f32[197,768]{1,0:T(8,128)}, f32[197,768]{1,0:T(8,128)}, f32[197,768]{1,0:T(8,128)}) async-done(((f32[197,768]{1,0:T(8,128)}, f32[197,768]{1,0:T(8,128)}, f32[197,768]{1,0:T(8,128)}, f32[197,768]{1,0:T(8,128)}), (f32[197,768]{1,0:T(8,128)}, f32[197,768]{1,0:T(8,128)}, f32[197,768]{1,0:T(8,128)}, ...) | async-done | bytes 2420752 | tf_op jit(solution)/shard_map/psum | solution.py:168
  887.6 4.5 fusion.170
  892.3 6.3 add_bitcast_fusion
  916.0 4.9 fusion.548
  928.4 4.0 copy.303
  932.4 4.4 reshape.1964
  946.2 4.1 add_bitcast_fusion.1
  957.4 28.3 %all-reduce.20.cloned.1.call-done = (f32[197,768]{1,0:T(8,128)}, f32[197,768]{1,0:T(8,128)}, f32[197,768]{1,0:T(8,128)}, f32[197,768]{1,0:T(8,128)}, f32[197,768...) async-done(((f32[197,768]{1,0:T(8,128)}, f32[197,768]{1,0:T(8,128)}, f32[197,768]{1,0:T(8,128)}, f32[197,768]{1,0:T(8,128)}, ...) | async-done | bytes 4841488 | tf_op jit(solution)/shard_map/psum | solution.py:124
  1001.9 4.9 pad_maximum_fusion.1
  1006.7 8.3 copy.245
  1035.0 9.3 copy.299
  1044.2 10.8 reshape.1960
  1083.4 21.9 %all-reduce = f32[2,2,3,64]{3,2,1,0:T(4,128)S(1)} all-reduce(f32[2,2,3,64]{3,2,1,0:T(4,128)S(1)} %pad_maximum_fusion.32), channel_id=19, replica_groups=mesh['dp'=8,'tensor'=4] {'dp'}, use_global_device_ids=true, to_apply=%region_137.0.clone | all-reduce | flops 768 | bytes 6144
  1108.0 4.7 multiply_bitcast_fusion.3
  1122.2 57.1 %reduce-scatter.28.cloned.1.call-done = f32[96,8]{1,0:T(8,128)} async-done(((f32[768,8]{1,0:T(8,128)}), f32[96,8]{1,0:T(8,128)}) %reduce-scatter.28.cloned.1.call-update) | async-done | bytes 3088
  1180.9 170.4 %all-reduce.18.cloned.1.call-done = f32[2,768,768]{1,0,2:T(2,128)} async-done(((f32[2,768,768]{1,0,2:T(2,128)}), f32[2,768,768]{1,0,2:T(2,128)}) %all-reduce.18.cloned.1.call-update) | async-done | bytes 4718608
  1353.3 80.2 %reduce-scatter.20.cloned.1.call-done = f32[96,1152]{1,0:T(8,128)} async-done(((f32[768,1152]{1,0:T(8,128)}), f32[96,1152]{1,0:T(8,128)}) %reduce-scatter.20.cloned.1.call-update) | async-done | bytes 442384
  1436.3 96.4 %reduce-scatter.18.cloned.1.call-done = f32[2,96,768]{2,1,0:T(8,128)} async-done(((f32[2,768,768]{2,1,0:T(8,128)}), f32[2,96,768]{2,1,0:T(8,128)}) %reduce-scatter.18.cloned.1.call-update) | async-done | bytes 589840 | tf_op jit(solution)/shard_map/reduce_scatter | solution.py:259
  (1387 shorter events, 340.6 us)
Async XLA Ops:
  8.0 284.0 %all-reduce.32.cloned.1.call-start = ((), (), s32[]{:S(2)}) async-start(), calls=%async_computation.23 | async-start | bytes 4915200 | tf_op jit(solution)/shard_map/psum | solution.py:120
  43.1 181.6 %copy-start.265 = (f32[1,1,3,64]{3,2,1,0:T(4,128)}, f32[1,1,3,64]{3,2,1,0:T(4,128)S(1)}, u32[]{:S(2)}) copy-start(f32[1,1,3,64]{3,2,1,0:T(4,128)S(1)} %copy.187) | copy-start | bytes 2308
  43.1 180.6 %copy-start.260 = (f32[1,1,3,64]{3,2,1,0:T(4,128)}, f32[1,1,3,64]{3,2,1,0:T(4,128)S(1)}, u32[]{:S(2)}) copy-start(f32[1,1,3,64]{3,2,1,0:T(4,128)S(1)} %copy.188) | copy-start | bytes 2308
  124.7 89.3 %copy-start.253 = (f32[768]{0:T(1024)}, f32[768]{0:T(1024)S(1)}, u32[]{:S(2)}) copy-start(f32[768]{0:T(1024)S(1)} %get-tuple-element.127) | copy-start | bytes 9220
  124.7 178.5 %copy-start.249 = (f32[768]{0:T(1024)}, f32[768]{0:T(1024)S(1)}, u32[]{:S(2)}) copy-start(f32[768]{0:T(1024)S(1)} %get-tuple-element.125) | copy-start | bytes 9220
  159.0 67.6 %copy-start.54 = (bf16[1,3,64,768]{3,2,1,0:T(8,128)(2,1)}, bf16[1,3,64,768]{3,2,1,0:T(8,128)(2,1)S(1)}, u32[]{:S(2)}) copy-start(bf16[1,3,64,768]{3,2,1,0:T(8,128)(2,1)S(1)} %copy.191) | copy-start | bytes 884740
  209.9 82.1 %copy-start.41 = (f32[1,197,768]{2,0,1:T(1,128)}, f32[1,197,768]{2,0,1:T(1,128)S(1)}, u32[]{:S(2)}) copy-start(f32[1,197,768]{2,0,1:T(1,128)S(1)} %get-tuple-element.215) | copy-start | bytes 1815556
  228.6 67.5 %all-gather.21.cloned.1.call-start = ((), (), s32[]{:S(2)}) async-start(), calls=%async_computation.7 | async-start | bytes 1327104 | tf_op jit(solution)/shard_map/all_gather | solution.py:61
  229.4 86.7 %all-gather.23.cloned.1.call-start = ((), (), s32[]{:S(2)}) async-start(), calls=%async_computation.8 | async-start | bytes 1327104 | tf_op jit(solution)/shard_map/all_gather | solution.py:63
  230.3 260.4 %all-reduce.30.cloned.1.call-start = ((), (), s32[]{:S(2)}) async-start(), calls=%async_computation.22 | async-start | bytes 4915200 | tf_op jit(solution)/shard_map/psum | solution.py:124
  294.6 196.2 %copy-start.3 = (f32[197,768]{1,0:T(8,128)}, f32[197,768]{1,0:T(8,128)S(1)}, u32[]{:S(2)}) copy-start(f32[197,768]{1,0:T(8,128)S(1)} %get-tuple-element.304) | copy-start | bytes 1815556
  326.4 242.7 %all-reduce.28.cloned.1.call-start = ((), (), s32[]{:S(2)}) async-start(), calls=%async_computation.21 | async-start | bytes 4915200 | tf_op jit(solution)/shard_map/psum | solution.py:120
  326.6 182.7 %copy-start.267 = (f32[1,1,3,64]{3,2,1,0:T(4,128)}, f32[1,1,3,64]{3,2,1,0:T(4,128)S(1)}, u32[]{:S(2)}) copy-start(f32[1,1,3,64]{3,2,1,0:T(4,128)S(1)} %copy.199) | copy-start | bytes 2308
  326.7 181.6 %copy-start.262 = (f32[1,1,3,64]{3,2,1,0:T(4,128)}, f32[1,1,3,64]{3,2,1,0:T(4,128)S(1)}, u32[]{:S(2)}) copy-start(f32[1,1,3,64]{3,2,1,0:T(4,128)S(1)} %copy.200) | copy-start | bytes 2308
  429.0 80.9 %copy-start.56 = (bf16[1,3,64,768]{3,2,1,0:T(8,128)(2,1)}, bf16[1,3,64,768]{3,2,1,0:T(8,128)(2,1)S(1)}, u32[]{:S(2)}) copy-start(bf16[1,3,64,768]{3,2,1,0:T(8,128)(2,1)S(1)} %copy.203) | copy-start | bytes 884740
  512.4 63.3 %all-gather.25.cloned.1.call-start = ((), (), s32[]{:S(2)}) async-start(), calls=%async_computation.9 | async-start | bytes 1327104 | tf_op jit(solution)/shard_map/all_gather | solution.py:61
  512.9 85.0 %all-gather.27.cloned.1.call-start = ((), (), s32[]{:S(2)}) async-start(), calls=%async_computation.10 | async-start | bytes 1327104 | tf_op jit(solution)/shard_map/all_gather | solution.py:63
  513.7 161.0 %all-reduce.26.cloned.1.call-start = ((), (), s32[]{:S(2)}) async-start(), calls=%async_computation.20 | async-start | bytes 4915200 | tf_op jit(solution)/shard_map/psum | solution.py:168
  618.1 56.5 %copy-start.15 = (f32[197,768]{1,0:T(8,128)S(1)}, f32[197,768]{1,0:T(8,128)}, u32[]{:S(2)}) copy-start(f32[197,768]{1,0:T(8,128)} %copy-done.13) | copy-start | bytes 1815556
  618.1 56.5 %copy-start.286 = (f32[197]{0:T(256)S(1)}, f32[197]{0:T(256)}, u32[]{:S(2)}) copy-start(f32[197]{0:T(256)} %copy-done.284) | copy-start | bytes 2368
  618.1 56.5 %copy-start.314 = (f32[197]{0:T(256)S(1)}, f32[197]{0:T(256)}, u32[]{:S(2)}) copy-start(f32[197]{0:T(256)} %copy-done.313) | copy-start | bytes 2368
  618.2 56.5 %copy-start.352 = (f32[197]{0:T(256)S(1)}, f32[197]{0:T(256)}, u32[]{:S(2)}) copy-start(f32[197]{0:T(256)} %add_rsqrt_fusion.8) | copy-start | bytes 2368
  618.2 56.5 %copy-start.363 = (f32[197]{0:T(256)S(1)}, f32[197]{0:T(256)}, u32[]{:S(2)}) copy-start(f32[197]{0:T(256)} %add_rsqrt_fusion.12) | copy-start | bytes 2368
  618.2 59.3 %copy-start.318 = (f32[197]{0:T(256)S(1)}, f32[197]{0:T(256)}, u32[]{:S(2)}) copy-start(f32[197]{0:T(256)} %copy-done.316) | copy-start | bytes 2368
  618.2 59.3 %copy-start.322 = (f32[197]{0:T(256)S(1)}, f32[197]{0:T(256)}, u32[]{:S(2)}) copy-start(f32[197]{0:T(256)} %copy-done.320) | copy-start | bytes 2368
  618.2 59.3 %copy-start.366 = (f32[197]{0:T(256)S(1)}, f32[197]{0:T(256)}, u32[]{:S(2)}) copy-start(f32[197]{0:T(256)} %add_rsqrt_fusion) | copy-start | bytes 2368
  618.2 59.3 %copy-start.369 = (f32[197]{0:T(256)S(1)}, f32[197]{0:T(256)}, u32[]{:S(2)}) copy-start(f32[197]{0:T(256)} %add_rsqrt_fusion.4) | copy-start | bytes 2368
  618.2 153.1 %all-reduce.24.cloned.1.call-start = ((), (), s32[]{:S(2)}) async-start(), calls=%async_computation.19 | async-start | bytes 4915200 | tf_op jit(solution)/shard_map/psum | solution.py:190
  713.3 58.1 %copy-start.278 = (f32[197]{0:T(256)S(1)}, f32[197]{0:T(256)}, u32[]{:S(2)}) copy-start(f32[197]{0:T(256)} %copy-done.277) | copy-start | bytes 2368
  713.3 58.1 %copy-start.282 = (f32[197]{0:T(256)S(1)}, f32[197]{0:T(256)}, u32[]{:S(2)}) copy-start(f32[197]{0:T(256)} %copy-done.281) | copy-start | bytes 2368
  713.3 58.1 %copy-start.346 = (f32[197]{0:T(256)S(1)}, f32[197]{0:T(256)}, u32[]{:S(2)}) copy-start(f32[197]{0:T(256)} %copy-done.345) | copy-start | bytes 2368
  713.3 58.1 %copy-start.349 = (f32[197]{0:T(256)S(1)}, f32[197]{0:T(256)}, u32[]{:S(2)}) copy-start(f32[197]{0:T(256)} %copy-done.348) | copy-start | bytes 2368
  713.3 138.0 %all-reduce.22.cloned.1.call-start = ((), (), s32[]{:S(2)}) async-start(), calls=%async_computation.18 | async-start | bytes 4915200 | tf_op jit(solution)/shard_map/psum | solution.py:168
  721.9 52.5 %copy-start.280 = (f32[197]{0:T(256)S(1)}, f32[197]{0:T(256)}, u32[]{:S(2)}) copy-start(f32[197]{0:T(256)} %copy-done.279) | copy-start | bytes 2368
  721.9 52.5 %copy-start.325 = (f32[197]{0:T(256)S(1)}, f32[197]{0:T(256)}, u32[]{:S(2)}) copy-start(f32[197]{0:T(256)} %copy-done.324) | copy-start | bytes 2368
  721.9 52.5 %copy-start.343 = (f32[197]{0:T(256)S(1)}, f32[197]{0:T(256)}, u32[]{:S(2)}) copy-start(f32[197]{0:T(256)} %copy-done.342) | copy-start | bytes 2368
  721.9 52.5 %copy-start.372 = (f32[197]{0:T(256)S(1)}, f32[197]{0:T(256)}, u32[]{:S(2)}) copy-start(f32[197]{0:T(256)} %copy-done.371) | copy-start | bytes 2368
  793.3 192.4 %all-reduce.20.cloned.1.call-start = ((), (), s32[]{:S(2)}) async-start(), calls=%async_computation.17 | async-start | bytes 9830400 | tf_op jit(solution)/shard_map/psum | solution.py:124
  805.6 45.8 %copy-start.12 = (f32[197,768]{1,0:T(8,128)S(1)}, f32[197,768]{1,0:T(8,128)}, u32[]{:S(2)}) copy-start(f32[197,768]{1,0:T(8,128)} %copy-done.10) | copy-start | bytes 1815556
  805.6 45.8 %copy-start.305 = (f32[197]{0:T(256)S(1)}, f32[197]{0:T(256)}, u32[]{:S(2)}) copy-start(f32[197]{0:T(256)} %copy-done.304) | copy-start | bytes 2368
  805.6 45.8 %copy-start.311 = (f32[197]{0:T(256)S(1)}, f32[197]{0:T(256)}, u32[]{:S(2)}) copy-start(f32[197]{0:T(256)} %copy-done.310) | copy-start | bytes 2368
  886.9 194.9 %reduce-scatter.24.cloned.1.call-start = ((), (), s32[]{:S(2)}) async-start(), calls=%async_computation.13 | async-start | bytes 73728
  920.9 185.1 %reduce-scatter.22.cloned.1.call-start = ((), (), s32[]{:S(2)}) async-start(), calls=%async_computation.12 | async-start | bytes 1327104
  936.8 183.8 %reduce-scatter.26.cloned.1.call-start = ((), (), s32[]{:S(2)}) async-start(), calls=%async_computation.14 | async-start | bytes 442368
  997.4 181.8 %reduce-scatter.28.cloned.1.call-start = ((), (), s32[]{:S(2)}) async-start(), calls=%async_computation.15 | async-start | bytes 442368
  1001.8 349.5 %all-reduce.18.cloned.1.call-start = ((), (), s32[]{:S(2)}) async-start(), calls=%async_computation.16 | async-start | bytes 9437184
  1015.1 418.4 %reduce-scatter.20.cloned.1.call-start = ((), (), s32[]{:S(2)}) async-start(), calls=%async_computation.11 | async-start | bytes 3981312
  1055.0 477.7 %reduce-scatter.18.cloned.1.call-start = ((), (), s32[]{:S(2)}) async-start(), calls=%async_computation.6 | async-start | bytes 5308416 | tf_op jit(solution)/shard_map/reduce_scatter | solution.py:259
  (454 other events, 2502.6 us)
Sparse Core Ops, SparseCore 0:
  228.8 57.9 all-reduce.31
  326.6 56.2 all-reduce.29
  512.5 56.6 all-reduce.27
  618.3 56.2 all-reduce.25
  713.4 57.8 all-reduce.23
  793.4 57.8 all-reduce.21
  887.0 98.6 all-reduce.19
Sparse Core Ops, SparseCore 1:
  231.9 41.5 all-gather.20
  276.1 40.0 all-gather.22
  515.0 39.9 all-gather.24
  557.8 40.1 all-gather.26
  921.0 62.0 reduce-scatter.23
  986.8 63.2 reduce-scatter.21
  1054.1 60.5 reduce-scatter.25
  1118.7 60.5 reduce-scatter.27
  1183.2 168.1 all-reduce.17
  1355.4 78.0 reduce-scatter.19
  1438.0 94.6 reduce-scatter.17
where the time goes:
time: 1550 us; the launch traced here: 1540 us
  waiting for transfers between devices  617 us (40%)
  blocking collectives  416 us (27%)
  matrix products  235 us (15%)
  local copies, waits for them, and re-layouts  163 us (11%)
  other arithmetic  82.8 us (5%)
  between operations  24.3 us (2%)
    unnamed x24, waiting for transfers between devices  309 us
    dot_general x96, matrix products, product(): return jnp.dot(a, b, precision=highest, preferred_element_type=jnp.float32)  188 us
    reduce_scatter x1, waiting for transfers between devices, shards(): lax.psum_scatter(up_total, 'dp', scatter_dimension=1, tiled=True)  96.4 us
    psum x2, waiting for transfers between devices, layer_backward(): grad_norm_two = lax.psum(product(grad_hidden, up_part.T), 'tensor')  94.8 us
    all_gather x2, blocking collectives, fetch_forward(): lax.all_gather(qkv_slice, 'dp', axis=0, tiled=True)  77.5 us
    unnamed x1007, local copies, waits for them, and re-layouts  71.5 us
    all_gather x2, blocking collectives, fetch_forward(): lax.all_gather(out_slice, 'dp', axis=2, tiled=True)  68.5 us
    all_gather x2, blocking collectives, fetch_forward(): lax.all_gather(bias_slice, 'dp', axis=2, tiled=True)  62.8 us
  transfers between devices with their start and end apart: 18, of which 11 were waited for; matrix products, arithmetic and copies ran while one was open for 18% of the time, Pallas kernels for 0%

commit v1 on v0

v1 whole, which is shorter than its diff:
```python
import math

import jax
import jax.numpy as jnp
from jax import lax
from jax.sharding import PartitionSpec as P

epsilon = 1e-06
high = lax.Precision.HIGH
f32 = jnp.float32
bf16 = jnp.bfloat16


def weight_product(a, w, w_dim=0):
    top = lax.reduce_precision(a, 8, 7)
    rest = (a - top).astype(bf16)
    dims = (((1,), (w_dim,)), ((), ()))
    return lax.dot_general(
        top.astype(bf16), w, dims, preferred_element_type=f32
    ) + lax.dot_general(rest, w, dims, preferred_element_type=f32)


def cross(a, b):
    return lax.dot_general(
        a, b, (((0,), (0,)), ((), ())), precision=high, preferred_element_type=f32
    )


def heads_product(spec, a, b):
    return jnp.einsum(spec, a, b, precision=high, preferred_element_type=f32)


def norm_keep(values, gain, shift):
    average = jnp.mean(values, axis=-1, keepdims=True)
    centered = values - average
    variance = jnp.mean(centered * centered, axis=-1, keepdims=True)
    inverse = lax.rsqrt(variance + epsilon)
    normed = centered * inverse
    return (normed * gain + shift, normed, inverse)


def norm_back(grad_out, normed, inverse, gain):
    scaled = grad_out * gain
    first_mean = jnp.mean(scaled, axis=-1, keepdims=True)
    second_mean = jnp.mean(scaled * normed, axis=-1, keepdims=True)
    return inverse * (scaled - first_mean - normed * second_mean)


def gelu_parts(hidden):
    normal_cdf = 0.5 * (1.0 + lax.erf(hidden / math.sqrt(2.0)))
    density = jnp.exp(-0.5 * hidden * hidden) / math.sqrt(2.0 * math.pi)
    return (hidden * normal_cdf, normal_cdf + hidden * density)


core_pairs = [(0, 1), (1, 0), (2, 3), (3, 2)]
chip_pairs = [(0, 2), (2, 0), (1, 3), (3, 1)]


def tensor_sum(partial):
    rows, width = partial.shape
    halves = partial.reshape(2, rows // 2, width)
    core = lax.rem(lax.axis_index("tensor"), 2)
    first = core == 0
    mine = jnp.where(first, halves[0], halves[1])
    other = jnp.where(first, halves[1], halves[0])
    mine = mine + lax.ppermute(other, "tensor", core_pairs)
    mine = mine + lax.ppermute(mine, "tensor", chip_pairs)
    other = lax.ppermute(mine, "tensor", core_pairs)
    return jnp.concatenate([jnp.where(first, mine, other), jnp.where(first, other, mine)])


def pack_small(rows_six, bias, up_bias):
    depth = rows_six.shape[1]
    flat = jnp.concatenate([bias.reshape(-1), up_bias.reshape(-1)])
    columns = -(-flat.shape[0] // depth)
    flat = jnp.pad(flat, (0, columns * depth - flat.shape[0])).reshape(columns, depth)
    block = jnp.concatenate([rows_six, flat]).T
    return jnp.pad(block, ((0, 0), (0, 128 - block.shape[1])))


def gather_weights(params, layer):
    qkv, bias, out, up, upb, down, gains, shifts = [p[layer] for p in params]
    depth, heads, head_dim = (qkv.shape[0], qkv.shape[2], qkv.shape[3])
    inner = heads * head_dim
    small = pack_small(jnp.concatenate([gains, shifts]), bias, upb)
    attention = jnp.concatenate(
        [qkv.reshape(depth, 3 * inner), out.reshape(inner, depth).T, small], axis=1
    )
    feed = jnp.concatenate([up, down.T], axis=1)
    attention = lax.all_gather(attention, "dp", axis=0, tiled=True)
    feed = lax.all_gather(feed, "dp", axis=0, tiled=True)
    width = attention.shape[0]
    n = width // depth
    small = attention[:, 4 * inner :].astype(f32).T
    bias_count, upb_count = (bias.size, upb.size)
    columns = -(-(bias_count + upb_count) // depth)
    flat = small[6 : 6 + columns].reshape(columns, n, depth).transpose(1, 0, 2).reshape(n, -1)
    bias_full = (
        flat[:, :bias_count]
        .reshape((n,) + bias.shape)
        .transpose(1, 2, 0, 3)
        .reshape(2, 1, inner)
    )
    upb_full = (
        flat[:, bias_count : bias_count + upb_count]
        .reshape((n,) + upb.shape)
        .transpose(1, 0, 2)
        .reshape(1, -1)
    )
    ff = up.shape[1]
    return dict(
        qkv=attention[:, : 3 * inner],
        out=attention[:, 3 * inner : 4 * inner],
        up=feed[:, :ff],
        down=feed[:, ff:],
        gains=small[:2],
        shifts=small[2:6],
        bias=bias_full,
        upb=upb_full,
        heads=heads,
        head_dim=head_dim,
    )


def layer_forward(stream, w, tokens, padded):
    heads, head_dim = (w["heads"], w["head_dim"])
    inner = heads * head_dim
    rows = stream.shape[0]
    split = (rows // padded, padded, heads, head_dim)
    factor = 1.0 / math.sqrt(head_dim)
    h, normed, inverse = norm_keep(stream, w["gains"][0], w["shifts"][0])
    projected = weight_product(h, w["qkv"])
    q = (projected[:, :inner] + w["bias"][0]).reshape(split)
    k = projected[:, inner : 2 * inner].reshape(split)
    v = (projected[:, 2 * inner :] + w["bias"][1]).reshape(split)
    scores = heads_product("bqhe,bkhe->bhqk", q, k) * factor
    live = lax.broadcasted_iota(jnp.int32, (1, 1, 1, padded), 3) < tokens
    scores = jnp.where(live, scores, -jnp.inf)
    exponent = jnp.exp(scores - jnp.max(scores, axis=-1, keepdims=True))
    soft = exponent / jnp.sum(exponent, axis=-1, keepdims=True)
    mixed = heads_product("bhqk,bkhe->bqhe", soft, v).reshape(rows, inner)
    middle = stream + tensor_sum(weight_product(mixed, w["out"], 1)) + w["shifts"][2]
    h2, normed_two, inverse_two = norm_keep(middle, w["gains"][1], w["shifts"][1])
    hidden = weight_product(h2, w["up"]) + w["upb"]
    activated, slope = gelu_parts(hidden)
    result = middle + tensor_sum(weight_product(activated, w["down"], 1)) + w["shifts"][3]
    return (
        result,
        (normed, inverse, h, q, k, v, soft, mixed, normed_two, inverse_two, h2, activated, slope),
    )


def backward_feed(grad, w, stored):
    normed_two, inverse_two, h2, activated, slope = stored[8:]
    grad_hidden = weight_product(grad, w["down"]) * slope
    grad_norm = tensor_sum(weight_product(grad_hidden, w["up"], 1))
    middle = grad + norm_back(grad_norm, normed_two, inverse_two, w["gains"][1])
    feed = jnp.concatenate([cross(h2, grad_hidden), cross(grad, activated)], axis=1)
    sums = (
        jnp.sum(grad_norm * normed_two, axis=0),
        jnp.sum(grad_norm, axis=0),
        jnp.sum(grad, axis=0),
        jnp.sum(grad_hidden, axis=0),
    )
    return (middle, feed, sums)


def backward_attention(grad, w, stored, padded):
    normed, inverse, h, q, k, v, soft, mixed = stored[:8]
    heads, head_dim = (w["heads"], w["head_dim"])
    inner = heads * head_dim
    rows = grad.shape[0]
    split = (rows // padded, padded, heads, head_dim)
    factor = 1.0 / math.sqrt(head_dim)
    grad_mixed = weight_product(grad, w["out"])
    out_delta = cross(grad, mixed)
    shift_two = jnp.sum(grad, axis=0)
    dots = jnp.sum((grad_mixed * mixed).reshape(split), axis=-1).transpose(0, 2, 1)[..., None]
    grad_mixed = grad_mixed.reshape(split)
    grad_soft = heads_product("bqhe,bkhe->bhqk", grad_mixed, v)
    grad_v = heads_product("bhqk,bqhe->bkhe", soft, grad_mixed).reshape(rows, inner)
    grad_scores = soft * (grad_soft - dots) * factor
    grad_q = heads_product("bhqk,bkhe->bqhe", grad_scores, k).reshape(rows, inner)
    grad_k = heads_product("bhqk,bqhe->bkhe", grad_scores, q).reshape(rows, inner)
    projected = jnp.concatenate([grad_q, grad_k, grad_v], axis=1)
    grad_norm = tensor_sum(weight_product(projected, w["qkv"], 1))
    qkv_delta = cross(h, projected)
    sums = (
        jnp.sum(grad_norm * normed, axis=0),
        jnp.sum(grad_norm, axis=0),
        shift_two,
        jnp.stack([jnp.sum(grad_q, axis=0), jnp.sum(grad_v, axis=0)]),
    )
    grad_in = grad + norm_back(grad_norm, normed, inverse, w["gains"][0])
    return (grad_in, jnp.concatenate([qkv_delta, out_delta], axis=1), sums)


def shards(
    images,
    counts,
    qkv_weight,
    qv_bias,
    out_weight,
    up_weight,
    up_bias,
    down_weight,
    gains,
    shifts,
    cotangent,
):
    params = (qkv_weight, qv_bias, out_weight, up_weight, up_bias, down_weight, gains, shifts)
    slots, tokens, width = images.shape
    layers, depth = qkv_weight.shape[:2]
    n = width // depth
    padded = -(-tokens // 8) * 8
    present = (jnp.arange(slots) < counts[0]).astype(f32)[:, None, None]
    groups = 2
    per = slots // groups
    extend = ((0, 0), (0, padded - tokens), (0, 0))
    x_all = jnp.pad(images, extend)
    g_all = jnp.pad(cotangent * present, extend)
    weights = [gather_weights(params, layer) for layer in range(layers)]
    streams = [x_all[g * per : (g + 1) * per].reshape(per * padded, width) for g in range(groups)]
    grads = [g_all[g * per : (g + 1) * per].reshape(per * padded, width) for g in range(groups)]
    kept = []
    for layer in range(layers):
        both = [layer_forward(s, weights[layer], tokens, padded) for s in streams]
        streams = [b[0] for b in both]
        kept.append([b[1] for b in both])
    totals = [None] * layers
    for layer in reversed(range(layers)):
        w = weights[layer]
        both = [backward_feed(g, w, s) for g, s in zip(grads, kept[layer])]
        feed_total = lax.psum_scatter(
            sum(b[1] for b in both[1:]) + both[0][1], "dp", scatter_dimension=0, tiled=True
        )
        gain_one, shift_one, shift_three, upb_grad = [
            both[0][2][i] + both[1][2][i] for i in range(4)
        ]
        both = [backward_attention(b[0], w, s, padded) for b, s in zip(both, kept[layer])]
        grads = [b[0] for b in both]
        gain_zero, shift_zero, shift_two, bias_grad = [
            both[0][2][i] + both[1][2][i] for i in range(4)
        ]
        six = jnp.stack([gain_zero, gain_one, shift_zero, shift_one, shift_two, shift_three])
        bias_shape = (2, w["heads"], n, w["head_dim"] // n)
        upb_shape = (up_bias.shape[1], n, up_bias.shape[2])
        flat = jnp.concatenate(
            [
                bias_grad.reshape(bias_shape).transpose(2, 0, 1, 3).reshape(n, -1),
                upb_grad.reshape(upb_shape).transpose(1, 0, 2).reshape(n, -1),
            ],
            axis=1,
        )
        columns = -(-flat.shape[1] // depth)
        flat = jnp.pad(flat, ((0, 0), (0, columns * depth - flat.shape[1])))
        flat = flat.reshape(n, columns, depth).transpose(1, 0, 2).reshape(columns, width)
        small = jnp.concatenate([six, flat]).T
        small = jnp.pad(small, ((0, 0), (0, 128 - small.shape[1])))
        attention_total = lax.psum_scatter(
            jnp.concatenate([both[0][1] + both[1][1], small], axis=1),
            "dp",
            scatter_dimension=0,
            tiled=True,
        )
        totals[layer] = (attention_total, feed_total)
    heads, head_dim = qkv_weight.shape[3:]
    inner = heads * head_dim
    ff = up_weight.shape[2]
    collected = []
    for attention, feed in totals:
        small = attention[:, 4 * inner : 4 * inner + 128].T
        bias_count, upb_count = (qv_bias[0].size, up_bias[0].size)
        columns = -(-(bias_count + upb_count) // depth)
        flat = small[6 : 6 + columns].reshape(-1)
        collected.append(
            (
                attention[:, : 3 * inner].reshape(qkv_weight.shape[1:]),
                flat[:bias_count].reshape(qv_bias.shape[1:]),
                attention[:, 3 * inner : 4 * inner].T.reshape(out_weight.shape[1:]),
                feed[:, :ff],
                flat[bias_count : bias_count + upb_count].reshape(up_bias.shape[1:]),
                feed[:, ff:].T,
                small[:2],
                small[2:6],
            )
        )
    joined = [
        jnp.concatenate([s.reshape(per, padded, width) for s in part])[:, :tokens]
        for part in (streams, grads)
    ]
    return (joined[0] * present, joined[1]) + tuple(
        jnp.stack([c[i] for c in collected]) for i in range(8)
    )


def solution(mesh):
    placed = (
        P("dp", None, None),
        P("dp"),
        P(None, "dp", None, "tensor", None),
        P(None, None, "tensor", "dp"),
        P(None, "tensor", None, "dp"),
        P(None, "dp", "tensor"),
        P(None, "tensor", "dp"),
        P(None, "tensor", "dp"),
        P(None, None, "dp"),
        P(None, None, "dp"),
        P("dp", None, None),
    )
    return jax.shard_map(
        shards,
        mesh=mesh,
        in_specs=placed,
        out_specs=(placed[0], placed[0]) + placed[2:10],
        check_vma=False,
    )
```

time: 1550 us -> 901 us (0.58)
  blocking collectives: 416 us -> 0 us
  waiting for transfers between devices: 617 us -> 303 us
  other arithmetic: 82.8 us -> 172 us
  matrix products: 235 us -> 151 us
  local copies, waits for them, and re-layouts: 163 us -> 216 us
  starting transfers between devices: 1.52 us -> 23.9 us
    all_gather x12 -> x0, blocking collectives: 395 us -> none  [the longest x2 77.5 us: fetch_forward(): lax.all_gather(qkv_slice, 'dp', axis=0, tiled=True)]
    psum x7 -> x0, waiting for transfers between devices: 188 us -> none  [the longest x2 94.8 us: layer_backward(): grad_norm_two = lax.psum(product(grad_hidden, up_part.T), 'tensor')]
    unnamed x24 -> x12, waiting for transfers between devices: 309 us -> 123 us
    ppermute x0 -> x48, waiting for transfers between devices: none -> 142 us  [the longest x16 142 us: tensor_sum(): mine = mine + lax.ppermute(mine, 'tensor', chip_pairs)]
    reduce_scatter x1 -> x0, waiting for transfers between devices: 96.4 us -> none  [shards(): lax.psum_scatter(up_total, 'dp', scatter_dimension=1, tiled=True)]
    dot_general x144 -> x104, matrix products: 235 us -> 151 us  [the longest x16 41.3 us: cross(): lax.dot_general(a, b, (((0,), (0,)), ((), ())), precision=high, preferred...]
    add x18 -> x59, other arithmetic: 3.1 us -> 74.1 us  [the longest x16 19.3 us: tensor_sum(): mine = mine + lax.ppermute(mine, 'tensor', chip_pairs)]
    reshape x0 -> x54, local copies, waits for them, and re-layouts: none -> 57.1 us  [the longest x4 8.2 us: backward_attention(): heads_product('bhqk,bqhe->bkhe', soft, grad_mixed).reshape(rows, inner)]
  transfers between devices with their start and end apart: 18 -> 56, of which waited for: 11 -> 18; matrix products, arithmetic and copies ran while one was open for 18% -> 50% of each run, Pallas kernels for 0% -> 0%
where the time goes in v1:
time: 901 us; the launch traced here: 886 us
  waiting for transfers between devices  303 us (34%)
  local copies, waits for them, and re-layouts  216 us (24%)
  other arithmetic  172 us (19%)
  matrix products  151 us (17%)
  starting transfers between devices  23.9 us (3%)
  between operations  19 us (2%)
    ppermute x16, waiting for transfers between devices, tensor_sum(): mine = mine + lax.ppermute(mine, 'tensor', chip_pairs)  142 us
    unnamed x12, waiting for transfers between devices  123 us
    unnamed x563, local copies, waits for them, and re-layouts  81.2 us
    dot_general x16, matrix products, cross(): lax.dot_general(a, b, (((0,), (0,)), ((), ())), precision=high, preferred...  41.3 us
    dot_general x24, matrix products, heads_product(): return jnp.einsum(spec, a, b, precision=high, preferred_element_type=f32)  40.3 us
    all_gather x2, waiting for transfers between devices, gather_weights(): attention = lax.all_gather(attention, 'dp', axis=0, tiled=True)  37.4 us
    dot_general x32, matrix products, weight_product(): lax.dot_general(top.astype(bf16), w, dims, preferred_element_type=f32)  36.3 us
    dot_general x32, matrix products, weight_product(): lax.dot_general(rest, w, dims, preferred_element_type=f32)  33.5 us
  transfers between devices with their start and end apart: 56, of which 18 were waited for; matrix products, arithmetic and copies ran while one was open for 50% of the time, Pallas kernels for 0%

profile of v1, /device:TPU:0, one launch (start us, length us, event | category | flops | bytes accessed | tf_op | source)
XLA Modules:
  0.0 885.6 jit_solution(16186916780232538564)
XLA Ops:
  21.4 37.4 %all-gather.5.cloned.1.call-done = bf16[768,896]{1,0:T(8,128)(2,1)} async-done(((bf16[96,896]{1,0:T(8,128)(2,1)}), bf16[768,896]{1,0:T(8,128)(2,1)}) %all-gather.5.cloned.1.call-update) | async-done | bytes 1376272 | tf_op jit(solution)/shard_map/all_gather | solution.py:90
  93.7 14.4 %collective-permute-done.1 = f32[200,768]{1,0:T(8,128)S(1)} collective-permute-done((f32[200,768]{1,0:T(8,128)S(1)}, f32[200,768]{1,0:T(8,128)S(1)}, u32[]{:S(2)}, u32[]{:S(2)}) %collective-permute-start.1) | collective-permute-done | bytes 614432 | tf_op jit(solution)/shard_map/ppermute | solution.py:67
  108.3 12.6 %collective-permute-done.13 = f32[200,768]{1,0:T(8,128)S(1)} collective-permute-done((f32[200,768]{1,0:T(8,128)S(1)}, f32[200,768]{1,0:T(8,128)S(1)}, u32[]{:S(2)}, u32[]{:S(2)}) %collective-permute-start.13) | collective-permute-done | bytes 614432 | tf_op jit(solution)/shard_map/ppermute | solution.py:67
  131.7 2.5 fusion.112
  154.1 12.8 %collective-permute-done.4 = f32[200,768]{1,0:T(8,128)} collective-permute-done((f32[200,768]{1,0:T(8,128)S(1)}, f32[200,768]{1,0:T(8,128)}, u32[]{:S(2)}, u32[]{:S(2)}) %collective-permute-start.4) | collective-permute-done | bytes 614432 | tf_op jit(solution)/shard_map/ppermute | solution.py:67
  172.1 7.0 collective-permute-done.16
  242.0 6.5 collective-permute-done.7
  250.7 3.5 fusion.123
  254.2 6.7 collective-permute-done.19
  282.4 3.0 subtract_multiply_fusion.3
  307.6 9.8 %collective-permute-done.10 = f32[200,768]{1,0:T(8,128)S(1)} collective-permute-done((f32[200,768]{1,0:T(8,128)S(1)}, f32[200,768]{1,0:T(8,128)S(1)}, u32[]{:S(2)}, u32[]{:S(2)}) %collective-permute-start.10) | collective-permute-done | bytes 614432 | tf_op jit(solution)/shard_map/ppermute | solution.py:67
  323.0 7.6 collective-permute-done.25
  332.1 5.1 fusion.82
  337.2 6.7 collective-permute-done.37
  345.2 11.3 %collective-permute-done.22 = f32[200,768]{1,0:T(8,128)} collective-permute-done((f32[200,768]{1,0:T(8,128)}, f32[200,768]{1,0:T(8,128)}, u32[]{:S(2)}, u32[]{:S(2)}) %collective-permute-start.22) | collective-permute-done | bytes 614432 | tf_op jit(solution)/shard_map/ppermute | solution.py:67
  372.9 4.9 multiply_add_fusion.12
  479.5 3.0 fusion.84
  482.5 4.4 collective-permute-done.40
  488.4 3.1 fusion.86
  496.2 5.2 fusion.332
  502.9 4.9 fusion.345
  512.8 3.2 maximum_add_fusion.3
  516.1 3.4 select_maximum_fusion
  519.5 3.3 copy.682
  523.5 3.9 multiply_add_fusion.10
  538.4 2.6 fusion.81
  546.0 11.9 %collective-permute-done.31 = f32[200,768]{1,0:T(8,128)S(1)} collective-permute-done((f32[200,768]{1,0:T(8,128)S(1)}, f32[200,768]{1,0:T(8,128)S(1)}, u32[]{:S(2)}, u32[]{:S(2)}) %collective-permute-start.31) | collective-permute-done | bytes 614432 | tf_op jit(solution)/shard_map/ppermute | solution.py:67
  558.1 2.7 fusion.327
  560.9 9.3 %collective-permute-done.43 = f32[200,768]{1,0:T(8,128)S(1)} collective-permute-done((f32[200,768]{1,0:T(8,128)S(1)}, f32[200,768]{1,0:T(8,128)S(1)}, u32[]{:S(2)}, u32[]{:S(2)}) %collective-permute-start.43) | collective-permute-done | bytes 614432 | tf_op jit(solution)/shard_map/ppermute | solution.py:67
  570.4 2.8 maximum_add_fusion.1
  573.2 6.1 copy.686
  584.2 4.5 multiply_add_fusion.8
  632.8 2.5 convolution_bitcast_fusion.1
  650.7 4.0 fusion.348
  654.8 4.5 fusion.398
  667.7 10.8 %collective-permute-done.34 = f32[200,768]{1,0:T(8,128)} collective-permute-done((f32[200,768]{1,0:T(8,128)}, f32[200,768]{1,0:T(8,128)}, u32[]{:S(2)}, u32[]{:S(2)}) %collective-permute-start.34) | collective-permute-done | bytes 614432 | tf_op jit(solution)/shard_map/ppermute | solution.py:67
  680.5 10.5 %collective-permute-done.46 = f32[200,768]{1,0:T(8,128)} collective-permute-done((f32[200,768]{1,0:T(8,128)}, f32[200,768]{1,0:T(8,128)}, u32[]{:S(2)}, u32[]{:S(2)}) %collective-permute-start.46) | collective-permute-done | bytes 614432 | tf_op jit(solution)/shard_map/ppermute | solution.py:67
  700.0 3.5 select_maximum_fusion.1
  703.4 3.3 copy.680
  707.0 4.3 fusion.404
  711.4 2.6 fusion.405
  714.0 2.7 fusion.85
  716.8 2.7 fusion.83
  719.5 2.7 maximum_add_fusion
  722.2 6.4 copy.684
  733.6 2.9 multiply_add_fusion.7
  744.0 32.7 %reduce-scatter.13.cloned.1.call-done = f32[96,896]{1,0:T(8,128)} async-done(((f32[768,896]{1,0:T(8,128)}), f32[96,896]{1,0:T(8,128)}) %reduce-scatter.13.cloned.1.call-update) | async-done | bytes 344080
  784.1 90.7 %reduce-scatter.17.cloned.1.call-done = f32[96,1536]{1,0:T(8,128)} async-done(((f32[768,1536]{1,0:T(8,128)}), f32[96,1536]{1,0:T(8,128)}) %reduce-scatter.17.cloned.1.call-update) | async-done | bytes 589840
  (1127 shorter events, 453.7 us)
Async XLA Ops:
  7.2 51.5 %all-gather.5.cloned.1.call-start = ((), (), s32[]{:S(2)}) async-start(), calls=%async_computation.4 | async-start | bytes 1548288 | tf_op jit(solution)/shard_map/all_gather | solution.py:90
  13.6 118.1 %all-gather.7.cloned.1.call-start = ((), (), s32[]{:S(2)}) async-start(), calls=%async_computation.5 | async-start | bytes 2654208 | tf_op jit(solution)/shard_map/all_gather | solution.py:91
  15.7 152.6 %all-gather.9.cloned.1.call-start = ((), (), s32[]{:S(2)}) async-start(), calls=%async_computation.6 | async-start | bytes 1548288 | tf_op jit(solution)/shard_map/all_gather | solution.py:90
  79.1 10.5 %collective-permute-start = (f32[200,768]{1,0:T(8,128)}, f32[200,768]{1,0:T(8,128)}, u32[]{:S(2)}, u32[]{:S(2)}) collective-permute-start(f32[200,768]{1,0:T(8,128)} %slice_select_fusion.15), channel_id=1, source_target_pairs={{0,1},{1,0},{2,3},{3,2},{4,5},{5,4},{6,7},{7,6},{8,9},{9,8},{10,11... | collective-permute-start | bytes 1843208 | tf_op jit(solution)/shard_map/ppermute | solution.py:66
  91.4 16.7 %collective-permute-start.1 = (f32[200,768]{1,0:T(8,128)S(1)}, f32[200,768]{1,0:T(8,128)S(1)}, u32[]{:S(2)}, u32[]{:S(2)}) collective-permute-start(f32[200,768]{1,0:T(8,128)S(1)} %select_add_fusion.15), channel_id=1, source_target_pairs={{0,2},{2,0},{1,3},{3,1},{4,6},{6,4},{5,7},{7,5},{8,10},{10,8},{9,1... | collective-permute-start | bytes 1843208 | tf_op jit(solution)/shard_map/ppermute | solution.py:67
  93.1 27.8 %collective-permute-start.13 = (f32[200,768]{1,0:T(8,128)S(1)}, f32[200,768]{1,0:T(8,128)S(1)}, u32[]{:S(2)}, u32[]{:S(2)}) collective-permute-start(f32[200,768]{1,0:T(8,128)S(1)} %select_add_fusion.11), channel_id=1, source_target_pairs={{0,2},{2,0},{1,3},{3,1},{4,6},{6,4},{5,7},{7,5},{8,10},{10,8},{9,1... | collective-permute-start | bytes 1843208 | tf_op jit(solution)/shard_map/ppermute | solution.py:67
  108.2 14.8 %collective-permute-start.2 = (f32[200,768]{1,0:T(8,128)S(1)}, f32[200,768]{1,0:T(8,128)}, u32[]{:S(2)}, u32[]{:S(2)}) collective-permute-start(f32[200,768]{1,0:T(8,128)S(1)} %add.1061), channel_id=1, source_target_pairs={{0,1},{1,0},{2,3},{3,2},{4,5},{5,4},{6,7},{7,6},{8,9},{9,8},{10,11... | collective-permute-start | bytes 1843208 | tf_op jit(solution)/shard_map/ppermute | solution.py:68
  122.7 128.0 %all-gather.11.cloned.1.call-start = ((), (), s32[]{:S(2)}) async-start(), calls=%async_computation.7 | async-start | bytes 2654208 | tf_op jit(solution)/shard_map/all_gather | solution.py:91
  139.2 8.5 collective-permute-start.3
  150.0 16.9 %collective-permute-start.4 = (f32[200,768]{1,0:T(8,128)S(1)}, f32[200,768]{1,0:T(8,128)}, u32[]{:S(2)}, u32[]{:S(2)}) collective-permute-start(f32[200,768]{1,0:T(8,128)S(1)} %select_add_fusion.14), channel_id=1, source_target_pairs={{0,2},{2,0},{1,3},{3,1},{4,6},{6,4},{5,7},{7,5},{8,10},{10,8},{9,1... | collective-permute-start | bytes 1843208 | tf_op jit(solution)/shard_map/ppermute | solution.py:67
  152.4 26.7 %collective-permute-start.16 = (f32[200,768]{1,0:T(8,128)}, f32[200,768]{1,0:T(8,128)}, u32[]{:S(2)}, u32[]{:S(2)}) collective-permute-start(f32[200,768]{1,0:T(8,128)} %select_add_fusion.10), channel_id=1, source_target_pairs={{0,2},{2,0},{1,3},{3,1},{4,6},{6,4},{5,7},{7,5},{8,10},{10,8},{9,1... | collective-permute-start | bytes 1843208 | tf_op jit(solution)/shard_map/ppermute | solution.py:67
  153.8 585.3 %reduce-scatter.15.cloned.1.call-start = ((), (), s32[]{:S(2)}) async-start(), calls=%async_computation.9 | async-start | bytes 3096576
  168.2 16.0 %collective-permute-start.5 = (f32[200,768]{1,0:T(8,128)S(1)}, f32[200,768]{1,0:T(8,128)}, u32[]{:S(2)}, u32[]{:S(2)}) collective-permute-start(f32[200,768]{1,0:T(8,128)S(1)} %add.1080), channel_id=1, source_target_pairs={{0,1},{1,0},{2,3},{3,2},{4,5},{5,4},{6,7},{7,6},{8,9},{9,8},{10,11... | collective-permute-start | bytes 1843208 | tf_op jit(solution)/shard_map/ppermute | solution.py:68
  216.3 13.0 %collective-permute-start.6 = (f32[200,768]{1,0:T(8,128)}, f32[200,768]{1,0:T(8,128)}, u32[]{:S(2)}, u32[]{:S(2)}) collective-permute-start(f32[200,768]{1,0:T(8,128)} %slice_select_fusion.13), channel_id=1, source_target_pairs={{0,1},{1,0},{2,3},{3,2},{4,5},{5,4},{6,7},{7,6},{8,9},{9,8},{10,11... | collective-permute-start | bytes 1843208 | tf_op jit(solution)/shard_map/ppermute | solution.py:66
  228.3 4.8 collective-permute-start.18
  231.5 17.0 %collective-permute-start.7 = (f32[200,768]{1,0:T(8,128)}, f32[200,768]{1,0:T(8,128)}, u32[]{:S(2)}, u32[]{:S(2)}) collective-permute-start(f32[200,768]{1,0:T(8,128)} %select_add_fusion.13), channel_id=1, source_target_pairs={{0,2},{2,0},{1,3},{3,1},{4,6},{6,4},{5,7},{7,5},{8,10},{10,8},{9,1... | collective-permute-start | bytes 1843208 | tf_op jit(solution)/shard_map/ppermute | solution.py:67
  234.0 26.9 %collective-permute-start.19 = (f32[200,768]{1,0:T(8,128)}, f32[200,768]{1,0:T(8,128)}, u32[]{:S(2)}, u32[]{:S(2)}) collective-permute-start(f32[200,768]{1,0:T(8,128)} %select_add_fusion.9), channel_id=1, source_target_pairs={{0,2},{2,0},{1,3},{3,1},{4,6},{6,4},{5,7},{7,5},{8,10},{10,8},{9,1... | collective-permute-start | bytes 1843208 | tf_op jit(solution)/shard_map/ppermute | solution.py:67
  250.7 13.3 %collective-permute-start.8 = (f32[200,768]{1,0:T(8,128)}, f32[200,768]{1,0:T(8,128)}, u32[]{:S(2)}, u32[]{:S(2)}) collective-permute-start(f32[200,768]{1,0:T(8,128)} %add.1101), channel_id=1, source_target_pairs={{0,1},{1,0},{2,3},{3,2},{4,5},{5,4},{6,7},{7,6},{8,9},{9,8},{10,11... | collective-permute-start | bytes 1843208 | tf_op jit(solution)/shard_map/ppermute | solution.py:68
  290.8 11.5 %collective-permute-start.24 = (f32[200,768]{1,0:T(8,128)S(1)}, f32[200,768]{1,0:T(8,128)S(1)}, u32[]{:S(2)}, u32[]{:S(2)}) collective-permute-start(f32[200,768]{1,0:T(8,128)S(1)} %slice_select_fusion.7), channel_id=1, source_target_pairs={{0,1},{1,0},{2,3},{3,2},{4,5},{5,4},{6,7},{7,6},{8,9},{9,8},{10,11... | collective-permute-start | bytes 1843208 | tf_op jit(solution)/shard_map/ppermute | solution.py:66
  296.6 7.1 collective-permute-start.36
  300.5 5.7 collective-permute-start.21
  300.7 16.7 %collective-permute-start.10 = (f32[200,768]{1,0:T(8,128)S(1)}, f32[200,768]{1,0:T(8,128)S(1)}, u32[]{:S(2)}, u32[]{:S(2)}) collective-permute-start(f32[200,768]{1,0:T(8,128)S(1)} %select_add_fusion.12), channel_id=1, source_target_pairs={{0,2},{2,0},{1,3},{3,1},{4,6},{6,4},{5,7},{7,5},{8,10},{10,8},{9,1... | collective-permute-start | bytes 1843208 | tf_op jit(solution)/shard_map/ppermute | solution.py:67
  303.2 27.5 %collective-permute-start.25 = (f32[200,768]{1,0:T(8,128)}, f32[200,768]{1,0:T(8,128)}, u32[]{:S(2)}, u32[]{:S(2)}) collective-permute-start(f32[200,768]{1,0:T(8,128)} %select_add_fusion.7), channel_id=1, source_target_pairs={{0,2},{2,0},{1,3},{3,1},{4,6},{6,4},{5,7},{7,5},{8,10},{10,8},{9,1... | collective-permute-start | bytes 1843208 | tf_op jit(solution)/shard_map/ppermute | solution.py:67
  304.6 39.2 %collective-permute-start.37 = (f32[200,768]{1,0:T(8,128)}, f32[200,768]{1,0:T(8,128)}, u32[]{:S(2)}, u32[]{:S(2)}) collective-permute-start(f32[200,768]{1,0:T(8,128)} %select_add_fusion.3), channel_id=1, source_target_pairs={{0,2},{2,0},{1,3},{3,1},{4,6},{6,4},{5,7},{7,5},{8,10},{10,8},{9,1... | collective-permute-start | bytes 1843208 | tf_op jit(solution)/shard_map/ppermute | solution.py:67
  307.1 49.5 %collective-permute-start.22 = (f32[200,768]{1,0:T(8,128)}, f32[200,768]{1,0:T(8,128)}, u32[]{:S(2)}, u32[]{:S(2)}) collective-permute-start(f32[200,768]{1,0:T(8,128)} %select_add_fusion.8), channel_id=1, source_target_pairs={{0,2},{2,0},{1,3},{3,1},{4,6},{6,4},{5,7},{7,5},{8,10},{10,8},{9,1... | collective-permute-start | bytes 1843208 | tf_op jit(solution)/shard_map/ppermute | solution.py:67
  318.3 40.5 %collective-permute-start.11 = (f32[200,768]{1,0:T(8,128)}, f32[200,768]{1,0:T(8,128)}, u32[]{:S(2)}, u32[]{:S(2)}) collective-permute-start(f32[200,768]{1,0:T(8,128)} %add.1120), channel_id=1, source_target_pairs={{0,1},{1,0},{2,3},{3,2},{4,5},{5,4},{6,7},{7,6},{8,9},{9,8},{10,11... | collective-permute-start | bytes 1843208 | tf_op jit(solution)/shard_map/ppermute | solution.py:68
  332.0 28.2 %collective-permute-start.26 = (f32[200,768]{1,0:T(8,128)S(1)}, f32[200,768]{1,0:T(8,128)S(1)}, u32[]{:S(2)}, u32[]{:S(2)}) collective-permute-start(f32[200,768]{1,0:T(8,128)S(1)} %add.1175), channel_id=1, source_target_pairs={{0,1},{1,0},{2,3},{3,2},{4,5},{5,4},{6,7},{7,6},{8,9},{9,8},{10,11... | collective-permute-start | bytes 1843208 | tf_op jit(solution)/shard_map/ppermute | solution.py:68
  345.2 15.8 %collective-permute-start.38 = (f32[200,768]{1,0:T(8,128)S(1)}, f32[200,768]{1,0:T(8,128)S(1)}, u32[]{:S(2)}, u32[]{:S(2)}) collective-permute-start(f32[200,768]{1,0:T(8,128)S(1)} %add.1200), channel_id=1, source_target_pairs={{0,1},{1,0},{2,3},{3,2},{4,5},{5,4},{6,7},{7,6},{8,9},{9,8},{10,11... | collective-permute-start | bytes 1843208 | tf_op jit(solution)/shard_map/ppermute | solution.py:68
  358.8 93.9 %collective-permute-start.23 = (f32[200,768]{1,0:T(8,128)}, f32[200,768]{1,0:T(8,128)}, u32[]{:S(2)}, u32[]{:S(2)}) collective-permute-start(f32[200,768]{1,0:T(8,128)} %add.1168), channel_id=1, source_target_pairs={{0,1},{1,0},{2,3},{3,2},{4,5},{5,4},{6,7},{7,6},{8,9},{9,8},{10,11... | collective-permute-start | bytes 1843208 | tf_op jit(solution)/shard_map/ppermute | solution.py:68
  424.1 31.0 %collective-permute-start.27 = (f32[200,768]{1,0:T(8,128)}, f32[200,768]{1,0:T(8,128)}, u32[]{:S(2)}, u32[]{:S(2)}) collective-permute-start(f32[200,768]{1,0:T(8,128)} %slice_select_fusion.6), channel_id=1, source_target_pairs={{0,1},{1,0},{2,3},{3,2},{4,5},{5,4},{6,7},{7,6},{8,9},{9,8},{10,11... | collective-permute-start | bytes 1843208 | tf_op jit(solution)/shard_map/ppermute | solution.py:66
  446.5 12.4 %collective-permute-start.39 = (f32[200,768]{1,0:T(8,128)}, f32[200,768]{1,0:T(8,128)}, u32[]{:S(2)}, u32[]{:S(2)}) collective-permute-start(f32[200,768]{1,0:T(8,128)} %slice_select_fusion.2), channel_id=1, source_target_pairs={{0,1},{1,0},{2,3},{3,2},{4,5},{5,4},{6,7},{7,6},{8,9},{9,8},{10,11... | collective-permute-start | bytes 1843208 | tf_op jit(solution)/shard_map/ppermute | solution.py:66
  457.3 20.5 %collective-permute-start.28 = (f32[200,768]{1,0:T(8,128)}, f32[200,768]{1,0:T(8,128)}, u32[]{:S(2)}, u32[]{:S(2)}) collective-permute-start(f32[200,768]{1,0:T(8,128)} %select_add_fusion.6), channel_id=1, source_target_pairs={{0,2},{2,0},{1,3},{3,1},{4,6},{6,4},{5,7},{7,5},{8,10},{10,8},{9,1... | collective-permute-start | bytes 1843208 | tf_op jit(solution)/shard_map/ppermute | solution.py:67
  460.9 26.0 %collective-permute-start.40 = (f32[200,768]{1,0:T(8,128)}, f32[200,768]{1,0:T(8,128)}, u32[]{:S(2)}, u32[]{:S(2)}) collective-permute-start(f32[200,768]{1,0:T(8,128)} %select_add_fusion.2), channel_id=1, source_target_pairs={{0,2},{2,0},{1,3},{3,1},{4,6},{6,4},{5,7},{7,5},{8,10},{10,8},{9,1... | collective-permute-start | bytes 1843208 | tf_op jit(solution)/shard_map/ppermute | solution.py:67
  479.2 12.2 %collective-permute-start.29 = (f32[200,768]{1,0:T(8,128)S(1)}, f32[200,768]{1,0:T(8,128)S(1)}, u32[]{:S(2)}, u32[]{:S(2)}) collective-permute-start(f32[200,768]{1,0:T(8,128)S(1)} %add.1181), channel_id=1, source_target_pairs={{0,1},{1,0},{2,3},{3,2},{4,5},{5,4},{6,7},{7,6},{8,9},{9,8},{10,11... | collective-permute-start | bytes 1843208 | tf_op jit(solution)/shard_map/ppermute | solution.py:68
  522.9 219.6 %reduce-scatter.19.cloned.1.call-start = ((), (), s32[]{:S(2)}) async-start(), calls=%async_computation.11 | async-start | bytes 5308416
  532.5 8.5 collective-permute-start.30
  537.1 5.7 collective-permute-start.42
  541.1 16.8 %collective-permute-start.31 = (f32[200,768]{1,0:T(8,128)S(1)}, f32[200,768]{1,0:T(8,128)S(1)}, u32[]{:S(2)}, u32[]{:S(2)}) collective-permute-start(f32[200,768]{1,0:T(8,128)S(1)} %select_add_fusion.5), channel_id=1, source_target_pairs={{0,2},{2,0},{1,3},{3,1},{4,6},{6,4},{5,7},{7,5},{8,10},{10,8},{9,1... | collective-permute-start | bytes 1843208 | tf_op jit(solution)/shard_map/ppermute | solution.py:67
  542.9 27.3 %collective-permute-start.43 = (f32[200,768]{1,0:T(8,128)S(1)}, f32[200,768]{1,0:T(8,128)S(1)}, u32[]{:S(2)}, u32[]{:S(2)}) collective-permute-start(f32[200,768]{1,0:T(8,128)S(1)} %select_add_fusion.1), channel_id=1, source_target_pairs={{0,2},{2,0},{1,3},{3,1},{4,6},{6,4},{5,7},{7,5},{8,10},{10,8},{9,1... | collective-permute-start | bytes 1843208 | tf_op jit(solution)/shard_map/ppermute | solution.py:67
  558.0 21.5 %collective-permute-start.32 = (f32[200,768]{1,0:T(8,128)S(1)}, f32[200,768]{1,0:T(8,128)S(1)}, u32[]{:S(2)}, u32[]{:S(2)}) collective-permute-start(f32[200,768]{1,0:T(8,128)S(1)} %add.1188), channel_id=1, source_target_pairs={{0,1},{1,0},{2,3},{3,2},{4,5},{5,4},{6,7},{7,6},{8,9},{9,8},{10,11... | collective-permute-start | bytes 1843208 | tf_op jit(solution)/shard_map/ppermute | solution.py:68
  570.3 9.4 %collective-permute-start.44 = (f32[200,768]{1,0:T(8,128)S(1)}, f32[200,768]{1,0:T(8,128)S(1)}, u32[]{:S(2)}, u32[]{:S(2)}) collective-permute-start(f32[200,768]{1,0:T(8,128)S(1)} %add.1213), channel_id=1, source_target_pairs={{0,1},{1,0},{2,3},{3,2},{4,5},{5,4},{6,7},{7,6},{8,9},{9,8},{10,11... | collective-permute-start | bytes 1843208 | tf_op jit(solution)/shard_map/ppermute | solution.py:68
  579.3 197.4 %reduce-scatter.13.cloned.1.call-start = ((), (), s32[]{:S(2)}) async-start(), calls=%async_computation.8 | async-start | bytes 3096576
  617.1 42.2 %collective-permute-start.33 = (f32[200,768]{1,0:T(8,128)}, f32[200,768]{1,0:T(8,128)}, u32[]{:S(2)}, u32[]{:S(2)}) collective-permute-start(f32[200,768]{1,0:T(8,128)} %slice_select_fusion.4), channel_id=1, source_target_pairs={{0,1},{1,0},{2,3},{3,2},{4,5},{5,4},{6,7},{7,6},{8,9},{9,8},{10,11... | collective-permute-start | bytes 1843208 | tf_op jit(solution)/shard_map/ppermute | solution.py:66
  649.8 13.2 %collective-permute-start.45 = (f32[200,768]{1,0:T(8,128)}, f32[200,768]{1,0:T(8,128)}, u32[]{:S(2)}, u32[]{:S(2)}) collective-permute-start(f32[200,768]{1,0:T(8,128)} %slice_select_fusion), channel_id=1, source_target_pairs={{0,1},{1,0},{2,3},{3,2},{4,5},{5,4},{6,7},{7,6},{8,9},{9,8},{10,11... | collective-permute-start | bytes 1843208 | tf_op jit(solution)/shard_map/ppermute | solution.py:66
  661.4 17.0 %collective-permute-start.34 = (f32[200,768]{1,0:T(8,128)}, f32[200,768]{1,0:T(8,128)}, u32[]{:S(2)}, u32[]{:S(2)}) collective-permute-start(f32[200,768]{1,0:T(8,128)} %select_add_fusion.4), channel_id=1, source_target_pairs={{0,2},{2,0},{1,3},{3,1},{4,6},{6,4},{5,7},{7,5},{8,10},{10,8},{9,1... | collective-permute-start | bytes 1843208 | tf_op jit(solution)/shard_map/ppermute | solution.py:67
  665.0 25.9 %collective-permute-start.46 = (f32[200,768]{1,0:T(8,128)}, f32[200,768]{1,0:T(8,128)}, u32[]{:S(2)}, u32[]{:S(2)}) collective-permute-start(f32[200,768]{1,0:T(8,128)} %select_add_fusion), channel_id=1, source_target_pairs={{0,2},{2,0},{1,3},{3,1},{4,6},{6,4},{5,7},{7,5},{8,10},{10,8},{9,1... | collective-permute-start | bytes 1843208 | tf_op jit(solution)/shard_map/ppermute | solution.py:67
  679.8 15.7 %collective-permute-start.35 = (f32[200,768]{1,0:T(8,128)S(1)}, f32[200,768]{1,0:T(8,128)S(1)}, u32[]{:S(2)}, u32[]{:S(2)}) collective-permute-start(f32[200,768]{1,0:T(8,128)S(1)} %add.1194), channel_id=1, source_target_pairs={{0,1},{1,0},{2,3},{3,2},{4,5},{5,4},{6,7},{7,6},{8,9},{9,8},{10,11... | collective-permute-start | bytes 1843208 | tf_op jit(solution)/shard_map/ppermute | solution.py:68
  706.8 168.0 %reduce-scatter.17.cloned.1.call-start = ((), (), s32[]{:S(2)}) async-start(), calls=%async_computation.10 | async-start | bytes 5308416
  (276 other events, 1468.6 us)
Sparse Core Ops, SparseCore 0:
  13.7 44.9 all-gather.4
  60.9 50.6 all-gather.6
  122.8 41.3 all-gather.8
  166.2 50.6 all-gather.10
  523.0 69.7 reduce-scatter.14
  596.3 94.3 reduce-scatter.18
  706.9 69.7 reduce-scatter.12
  780.3 94.4 reduce-scatter.16

commit v2 on v1

--- a/solution.py
+++ b/solution.py
@@ -3,6 +3,8 @@
 import jax
 import jax.numpy as jnp
 from jax import lax
+from jax.experimental import pallas as pl
+from jax.experimental.pallas import tpu as pltpu
 from jax.sharding import PartitionSpec as P
 
 epsilon = 1e-06
@@ -26,8 +28,80 @@
     )
 
 
-def heads_product(spec, a, b):
-    return jnp.einsum(spec, a, b, precision=high, preferred_element_type=f32)
+def halves_of(a):
+    top = a.astype(bf16)
+    return (top, (a - top.astype(f32)).astype(bf16))
+
+
+def split_dot(a, b, a_dim, b_dim):
+    dims = (((a_dim,), (b_dim,)), ((), ()))
+    dot = lambda x, y: lax.dot_general(x, y, dims, preferred_element_type=f32)
+    return dot(a[0], b[0]) + (dot(a[0], b[1]) + dot(a[1], b[0]))
+
+
+def soft_of(q, k, factor, tokens):
+    scores = split_dot(q, k, 1, 1) * factor
+    live = lax.broadcasted_iota(jnp.int32, scores.shape, 1) < tokens
+    scores = jnp.where(live, scores, -jnp.inf)
+    exponent = jnp.exp(scores - jnp.max(scores, axis=-1, keepdims=True))
+    return exponent / jnp.sum(exponent, axis=-1, keepdims=True)
+
+
+def attention_kernel(heads, head_dim, tokens, x_ref, bias_ref, o_ref):
+    inner = heads * head_dim
+    factor = 1.0 / math.sqrt(head_dim)
+    for j in range(heads):
+        at = slice(j * head_dim, (j + 1) * head_dim)
+        part = lambda i: x_ref[:, i * inner + j * head_dim : i * inner + (j + 1) * head_dim]
+        q = halves_of(part(0) + bias_ref[0:1, at])
+        k = halves_of(part(1))
+        v = halves_of(part(2) + bias_ref[1:2, at])
+        soft = soft_of(q, k, factor, tokens)
+        o_ref[:, at] = split_dot(halves_of(soft), v, 1, 0)
+
+
+def attention_back_kernel(heads, head_dim, tokens, x_ref, bias_ref, o_ref, g_ref, d_ref):
+    inner = heads * head_dim
+    factor = 1.0 / math.sqrt(head_dim)
+    for j in range(heads):
+        at = slice(j * head_dim, (j + 1) * head_dim)
+        part = lambda i: x_ref[:, i * inner + j * head_dim : i * inner + (j + 1) * head_dim]
+        q = halves_of(part(0) + bias_ref[0:1, at])
+        k = halves_of(part(1))
+        v = halves_of(part(2) + bias_ref[1:2, at])
+        soft = soft_of(q, k, factor, tokens)
+        grad = g_ref[:, at]
+        dots = jnp.sum(grad * o_ref[:, at], axis=-1, keepdims=True)
+        grad = halves_of(grad)
+        d_soft = split_dot(grad, v, 1, 1)
+        d_scores = halves_of(soft * (d_soft - dots) * factor)
+        d_ref[:, j * head_dim : (j + 1) * head_dim] = split_dot(d_scores, k, 1, 0)
+        d_ref[:, inner + j * head_dim : inner + (j + 1) * head_dim] = split_dot(d_scores, q, 0, 0)
+        d_ref[:, 2 * inner + j * head_dim : 2 * inner + (j + 1) * head_dim] = split_dot(
+            halves_of(soft), grad, 0, 0
+        )
+
+
+def attention_call(kernel, arrays, bias, width, w, tokens, padded, products):
+    rows = arrays[0].shape[0]
+    heads, head_dim = (w["heads"], w["head_dim"])
+    block = lambda n: pl.BlockSpec((padded, n), lambda i: (i, 0))
+    images = rows // padded
+    specs = [block(x.shape[1]) for x in arrays]
+    specs.insert(1, pl.BlockSpec(bias.shape, lambda i: (0, 0)))
+    return pl.pallas_call(
+        lambda *refs: kernel(heads, head_dim, tokens, *refs),
+        grid=(images,),
+        in_specs=specs,
+        out_specs=block(width),
+        out_shape=jax.ShapeDtypeStruct((rows, width), f32),
+        compiler_params=pltpu.CompilerParams(vmem_limit_bytes=32 * 1024 * 1024),
+        cost_estimate=pl.CostEstimate(
+            flops=products * 6 * images * heads * padded * padded * 2 * head_dim,
+            bytes_accessed=4 * rows * (4 * heads * head_dim + width),
+            transcendentals=images * heads * padded * padded,
+        ),
+    )(arrays[0], bias, *arrays[1:])
 
 
 def norm_keep(values, gain, shift):
@@ -57,16 +131,16 @@
 
 
 def tensor_sum(partial):
-    rows, width = partial.shape
-    halves = partial.reshape(2, rows // 2, width)
-    core = lax.rem(lax.axis_index("tensor"), 2)
-    first = core == 0
-    mine = jnp.where(first, halves[0], halves[1])
-    other = jnp.where(first, halves[1], halves[0])
-    mine = mine + lax.ppermute(other, "tensor", core_pairs)
+    half = partial.shape[0] // 2
+    mine = partial[:half] + lax.ppermute(partial[half:], "tensor", core_pairs)
     mine = mine + lax.ppermute(mine, "tensor", chip_pairs)
-    other = lax.ppermute(mine, "tensor", core_pairs)
-    return jnp.concatenate([jnp.where(first, mine, other), jnp.where(first, other, mine)])
+    return jnp.concatenate([mine, lax.ppermute(mine, "tensor", core_pairs)])
+
+
+def core_order(rows, first):
+    half = rows.shape[0] // 2
+    top, rest = (rows[:half], rows[half:])
+    return jnp.concatenate([jnp.where(first, top, rest), jnp.where(first, rest, top)])
 
 
 def pack_small(rows_six, bias, up_bias):
@@ -99,7 +173,7 @@
         flat[:, :bias_count]
         .reshape((n,) + bias.shape)
         .transpose(1, 2, 0, 3)
-        .reshape(2, 1, inner)
+        .reshape(2, inner)
     )
     upb_full = (
         flat[:, bias_count : bias_count + upb_count]
@@ -126,19 +200,11 @@
     heads, head_dim = (w["heads"], w["head_dim"])
     inner = heads * head_dim
     rows = stream.shape[0]
-    split = (rows // padded, padded, heads, head_dim)
-    factor = 1.0 / math.sqrt(head_dim)
     h, normed, inverse = norm_keep(stream, w["gains"][0], w["shifts"][0])
     projected = weight_product(h, w["qkv"])
-    q = (projected[:, :inner] + w["bias"][0]).reshape(split)
-    k = projected[:, inner : 2 * inner].reshape(split)
-    v = (projected[:, 2 * inner :] + w["bias"][1]).reshape(split)
-    scores = heads_product("bqhe,bkhe->bhqk", q, k) * factor
-    live = lax.broadcasted_iota(jnp.int32, (1, 1, 1, padded), 3) < tokens
-    scores = jnp.where(live, scores, -jnp.inf)
-    exponent = jnp.exp(scores - jnp.max(scores, axis=-1, keepdims=True))
-    soft = exponent / jnp.sum(exponent, axis=-1, keepdims=True)
-    mixed = heads_product("bhqk,bkhe->bqhe", soft, v).reshape(rows, inner)
+    mixed = attention_call(
+        attention_kernel, [projected], w["bias"], inner, w, tokens, padded, 2
+    )
     middle = stream + tensor_sum(weight_product(mixed, w["out"], 1)) + w["shifts"][2]
     h2, normed_two, inverse_two = norm_keep(middle, w["gains"][1], w["shifts"][1])
     hidden = weight_product(h2, w["up"]) + w["upb"]
@@ -146,12 +212,12 @@
     result = middle + tensor_sum(weight_product(activated, w["down"], 1)) + w["shifts"][3]
     return (
         result,
-        (normed, inverse, h, q, k, v, soft, mixed, normed_two, inverse_two, h2, activated, slope),
+        (normed, inverse, h, projected, mixed, normed_two, inverse_two, h2, activated, slope),
     )
 
 
 def backward_feed(grad, w, stored):
-    normed_two, inverse_two, h2, activated, slope = stored[8:]
+    normed_two, inverse_two, h2, activated, slope = stored[5:]
     grad_hidden = weight_product(grad, w["down"]) * slope
     grad_norm = tensor_sum(weight_product(grad_hidden, w["up"], 1))
     middle = grad + norm_back(grad_norm, normed_two, inverse_two, w["gains"][1])
@@ -165,31 +231,30 @@
     return (middle, feed, sums)
 
 
-def backward_attention(grad, w, stored, padded):
-    normed, inverse, h, q, k, v, soft, mixed = stored[:8]
+def backward_attention(grad, w, stored, tokens, padded):
+    normed, inverse, h, projected, mixed = stored[:5]
     heads, head_dim = (w["heads"], w["head_dim"])
     inner = heads * head_dim
-    rows = grad.shape[0]
-    split = (rows // padded, padded, heads, head_dim)
-    factor = 1.0 / math.sqrt(head_dim)
     grad_mixed = weight_product(grad, w["out"])
     out_delta = cross(grad, mixed)
     shift_two = jnp.sum(grad, axis=0)
-    dots = jnp.sum((grad_mixed * mixed).reshape(split), axis=-1).transpose(0, 2, 1)[..., None]
-    grad_mixed = grad_mixed.reshape(split)
-    grad_soft = heads_product("bqhe,bkhe->bhqk", grad_mixed, v)
-    grad_v = heads_product("bhqk,bqhe->bkhe", soft, grad_mixed).reshape(rows, inner)
-    grad_scores = soft * (grad_soft - dots) * factor
-    grad_q = heads_product("bhqk,bkhe->bqhe", grad_scores, k).reshape(rows, inner)
-    grad_k = heads_product("bhqk,bqhe->bkhe", grad_scores, q).reshape(rows, inner)
-    projected = jnp.concatenate([grad_q, grad_k, grad_v], axis=1)
+    projected = attention_call(
+        attention_back_kernel,
+        [projected, mixed, grad_mixed],
+        w["bias"],
+        3 * inner,
+        w,
+        tokens,
+        padded,
+        5,
+    )
     grad_norm = tensor_sum(weight_product(projected, w["qkv"], 1))
     qkv_delta = cross(h, projected)
     sums = (
         jnp.sum(grad_norm * normed, axis=0),
         jnp.sum(grad_norm, axis=0),
         shift_two,
-        jnp.stack([jnp.sum(grad_q, axis=0), jnp.sum(grad_v, axis=0)]),
+        jnp.sum(projected, axis=0).reshape(3, inner)[::2],
     )
     grad_in = grad + norm_back(grad_norm, normed, inverse, w["gains"][0])
     return (grad_in, jnp.concatenate([qkv_delta, out_delta], axis=1), sums)
@@ -217,11 +282,12 @@
     groups = 2
     per = slots // groups
     extend = ((0, 0), (0, padded - tokens), (0, 0))
+    first = lax.rem(lax.axis_index("tensor"), 2) == 0
     x_all = jnp.pad(images, extend)
     g_all = jnp.pad(cotangent * present, extend)
     weights = [gather_weights(params, layer) for layer in range(layers)]
-    streams = [x_all[g * per : (g + 1) * per].reshape(per * padded, width) for g in range(groups)]
-    grads = [g_all[g * per : (g + 1) * per].reshape(per * padded, width) for g in range(groups)]
+    streams = [core_order(x_all[g * per : (g + 1) * per], first).reshape(per * padded, width) for g in range(groups)]
+    grads = [core_order(g_all[g * per : (g + 1) * per], first).reshape(per * padded, width) for g in range(groups)]
     kept = []
     for layer in range(layers):
         both = [layer_forward(s, weights[layer], tokens, padded) for s in streams]
@@ -231,13 +297,14 @@
     for layer in reversed(range(layers)):
         w = weights[layer]
         both = [backward_feed(g, w, s) for g, s in zip(grads, kept[layer])]
-        feed_total = lax.psum_scatter(
-            sum(b[1] for b in both[1:]) + both[0][1], "dp", scatter_dimension=0, tiled=True
-        )
+        feed, middles = lax.optimization_barrier(
+            (both[0][1] + both[1][1], [b[0] for b in both])
+        )
+        feed_total = lax.psum_scatter(feed, "dp", scatter_dimension=0, tiled=True)
         gain_one, shift_one, shift_three, upb_grad = [
             both[0][2][i] + both[1][2][i] for i in range(4)
         ]
-        both = [backward_attention(b[0], w, s, padded) for b, s in zip(both, kept[layer])]
+        both = [backward_attention(m, w, s, tokens, padded) for m, s in zip(middles, kept[layer])]
         grads = [b[0] for b in both]
         gain_zero, shift_zero, shift_two, bias_grad = [
             both[0][2][i] + both[1][2][i] for i in range(4)
@@ -286,7 +353,7 @@
             )
         )
     joined = [
-        jnp.concatenate([s.reshape(per, padded, width) for s in part])[:, :tokens]
+        jnp.concatenate([core_order(s.reshape(per, padded, width), first) for s in part])[:, :tokens]
         for part in (streams, grads)
     ]
     return (joined[0] * present, joined[1]) + tuple(

time: 901 us -> 757 us (0.84)
  local copies, waits for them, and re-layouts: 216 us -> 83.6 us
  waiting for transfers between devices: 303 us -> 382 us
  other arithmetic: 172 us -> 94.6 us
  matrix products: 151 us -> 101 us
  Pallas kernels: 0 us -> 41.8 us
    reshape x36 -> x4, local copies, waits for them, and re-layouts: 49.1 us -> 0.31 us  [backward_attention(): jnp.sum(projected, axis=0).reshape(3, inner)[::2]]
    unnamed x12, waiting for transfers between devices: 123 us -> 169 us
    pallas_call x0 -> x8, Pallas kernels: none -> 41.8 us  [attention_call(): pl.pallas_call(lambda *refs: kernel(heads, head_dim, tokens, *refs), grid...]
    dot_general x24 -> x0, matrix products: 40.3 us -> none  [heads_product(): return jnp.einsum(spec, a, b, precision=high, preferred_element_type=f32)]
    unnamed x563 -> x237, local copies, waits for them, and re-layouts: 81.2 us -> 51.1 us
    add x24 -> x16, other arithmetic: 36.7 us -> 8.74 us  [tensor_sum(): mine = partial[:half] + lax.ppermute(partial[half:], 'tensor', core_pairs)]
    ppermute x16, waiting for transfers between devices: 142 us -> 170 us  [tensor_sum(): mine = mine + lax.ppermute(mine, 'tensor', chip_pairs)]
    transpose x20 -> x2, local copies, waits for them, and re-layouts: 20.7 us -> 0.01 us  [gather_weights(): bias_full = flat[:, :bias_count].reshape((n,) + bias.shape).transpose(1,...]
  transfers between devices with their start and end apart: 56 -> 56, of which waited for: 18 -> 27; matrix products, arithmetic and copies ran while one was open for 50% -> 29% of each run, Pallas kernels for 0% -> 4%
where the time goes in v2:
time: 757 us; the launch traced here: 747 us
  waiting for transfers between devices  382 us (50%)
  matrix products  101 us (13%)
  other arithmetic  94.6 us (12%)
  local copies, waits for them, and re-layouts  83.6 us (11%)
  Pallas kernels  41.8 us (6%)
  starting transfers between devices  26.1 us (3%)
  between operations  17.9 us (2%)
    ppermute x16, waiting for transfers between devices, tensor_sum(): mine = mine + lax.ppermute(mine, 'tensor', chip_pairs)  170 us
    unnamed x12, waiting for transfers between devices  169 us
    unnamed x237, local copies, waits for them, and re-layouts  51.1 us
    dot_general x16, matrix products, cross(): lax.dot_general(a, b, (((0,), (0,)), ((), ())), precision=high, preferred...  46.5 us
    pallas_call x8, Pallas kernels, attention_call(): pl.pallas_call(lambda *refs: kernel(heads, head_dim, tokens, *refs), grid...  41.8 us
    all_gather x2, waiting for transfers between devices, gather_weights(): attention = lax.all_gather(attention, 'dp', axis=0, tiled=True)  38.3 us
    dot_general x32, matrix products, weight_product(): lax.dot_general(rest, w, dims, preferred_element_type=f32)  27.3 us
    dot_general x32, matrix products, weight_product(): lax.dot_general(top.astype(bf16), w, dims, preferred_element_type=f32)  26.9 us
  transfers between devices with their start and end apart: 56, of which 27 were waited for; matrix products, arithmetic and copies ran while one was open for 29% of the time, Pallas kernels for 4%

profile of v2, /device:TPU:0, one launch (start us, length us, event | category | flops | bytes accessed | tf_op | source)
XLA Modules:
  0.0 746.7 jit_solution(18394121692328556320)
XLA Ops:
  22.2 36.6 %all-gather.5.cloned.1.call-done = bf16[768,896]{1,0:T(8,128)(2,1)} async-done(((bf16[96,896]{1,0:T(8,128)(2,1)}), bf16[768,896]{1,0:T(8,128)(2,1)}) %all-gather.5.cloned.1.call-update) | async-done | bytes 1376272 | tf_op jit(solution)/shard_map/all_gather | solution.py:164
  64.3 3.3 shard_map.188.refs_2_
  71.2 3.3 shard_map.186.refs_2_
  79.3 13.1 %collective-permute-done.13 = f32[200,768]{1,0:T(8,128)S(1)} collective-permute-done((f32[200,768]{1,0:T(8,128)S(1)}, f32[200,768]{1,0:T(8,128)S(1)}, u32[]{:S(2)}, u32[]{:S(2)}) %collective-permute-start.13) | collective-permute-done | bytes 614432 | tf_op jit(solution)/shard_map/ppermute | solution.py:136
  92.6 12.6 %collective-permute-done.1 = f32[200,768]{1,0:T(8,128)S(1)} collective-permute-done((f32[200,768]{1,0:T(8,128)S(1)}, f32[200,768]{1,0:T(8,128)S(1)}, u32[]{:S(2)}, u32[]{:S(2)}) %collective-permute-start.1) | collective-permute-done | bytes 614432 | tf_op jit(solution)/shard_map/ppermute | solution.py:136
  107.6 2.7 fusion.49
  126.7 13.6 %collective-permute-done.16 = f32[200,768]{1,0:T(8,128)S(1)} collective-permute-done((f32[200,768]{1,0:T(8,128)S(1)}, f32[200,768]{1,0:T(8,128)S(1)}, u32[]{:S(2)}, u32[]{:S(2)}) %collective-permute-start.16) | collective-permute-done | bytes 614432 | tf_op jit(solution)/shard_map/ppermute | solution.py:136
  141.1 11.4 %collective-permute-done.4 = f32[200,768]{1,0:T(8,128)S(1)} collective-permute-done((f32[200,768]{1,0:T(8,128)S(1)}, f32[200,768]{1,0:T(8,128)S(1)}, u32[]{:S(2)}, u32[]{:S(2)}) %collective-permute-start.4) | collective-permute-done | bytes 614432 | tf_op jit(solution)/shard_map/ppermute | solution.py:136
  159.9 3.4 slice_reduce_fusion
  167.5 3.3 shard_map.189.refs_2_
  173.8 12.1 %shard_map.187.refs_2_ = f32[400,192]{1,0:T(8,128)S(1)} custom-call(f32[400,576]{1,0:T(8,128)S(1)} %convolution_add_fusion.26.refs_0_, f32[2,192]{1,0:T(2,128)S(1)} %reshape.1988.refs_1_), custom_call_target="tpu_custom_call" | custom-call | flops 368640000 | bytes 1536000 | tf_op jit(solution)/shard_map/pallas_call | solution.py:92
  194.0 11.0 %collective-permute-done.19 = f32[200,768]{1,0:T(8,128)} collective-permute-done((f32[200,768]{1,0:T(8,128)S(1)}, f32[200,768]{1,0:T(8,128)}, u32[]{:S(2)}, u32[]{:S(2)}) %collective-permute-start.19) | collective-permute-done | bytes 614432 | tf_op jit(solution)/shard_map/ppermute | solution.py:136
  207.1 10.2 %collective-permute-done.7 = f32[200,768]{1,0:T(8,128)} collective-permute-done((f32[200,768]{1,0:T(8,128)S(1)}, f32[200,768]{1,0:T(8,128)}, u32[]{:S(2)}, u32[]{:S(2)}) %collective-permute-start.7) | collective-permute-done | bytes 614432 | tf_op jit(solution)/shard_map/ppermute | solution.py:136
  234.1 2.9 fusion.66
  255.1 11.4 %collective-permute-done.28 = f32[200,768]{1,0:T(8,128)S(1)} collective-permute-done((f32[200,768]{1,0:T(8,128)S(1)}, f32[200,768]{1,0:T(8,128)S(1)}, u32[]{:S(2)}, u32[]{:S(2)}) %collective-permute-start.28) | collective-permute-done | bytes 614432 | tf_op jit(solution)/shard_map/ppermute | solution.py:136
  266.8 2.9 maximum_add_fusion
  269.6 10.2 %collective-permute-done.10 = f32[200,768]{1,0:T(8,128)} collective-permute-done((f32[200,768]{1,0:T(8,128)S(1)}, f32[200,768]{1,0:T(8,128)}, u32[]{:S(2)}, u32[]{:S(2)}) %collective-permute-start.10) | collective-permute-done | bytes 614432 | tf_op jit(solution)/shard_map/ppermute | solution.py:136
  281.1 11.9 %collective-permute-done.22 = f32[200,768]{1,0:T(8,128)} collective-permute-done((f32[200,768]{1,0:T(8,128)}, f32[200,768]{1,0:T(8,128)}, u32[]{:S(2)}, u32[]{:S(2)}) %collective-permute-start.22) | collective-permute-done | bytes 614432 | tf_op jit(solution)/shard_map/ppermute | solution.py:136
  294.4 10.8 %collective-permute-done.25 = f32[200,768]{1,0:T(8,128)} collective-permute-done((f32[200,768]{1,0:T(8,128)S(1)}, f32[200,768]{1,0:T(8,128)}, u32[]{:S(2)}, u32[]{:S(2)}) %collective-permute-start.25) | collective-permute-done | bytes 614432 | tf_op jit(solution)/shard_map/ppermute | solution.py:136
  315.5 4.9 shard_map.190
  324.7 5.0 shard_map.191
  336.3 3.1 fusion.322
  349.3 4.5 fusion.69
  353.9 4.6 collective-permute-done.34
  360.6 10.4 %collective-permute-done.31 = f32[200,768]{1,0:T(8,128)} collective-permute-done((f32[200,768]{1,0:T(8,128)}, f32[200,768]{1,0:T(8,128)}, u32[]{:S(2)}, u32[]{:S(2)}) %collective-permute-start.31) | collective-permute-done | bytes 614432 | tf_op jit(solution)/shard_map/ppermute | solution.py:136
  374.1 3.5 fusion.65
  381.8 2.8 multiply_reduce_fusion.2
  384.7 3.7 fusion.282
  388.5 3.4 select_maximum_fusion
  391.9 3.3 copy.204
  395.2 6.1 copy.208
  406.5 2.7 fusion.64
  419.4 2.9 fusion.68
  427.7 11.4 %collective-permute-done.40 = f32[200,768]{1,0:T(8,128)S(1)} collective-permute-done((f32[200,768]{1,0:T(8,128)S(1)}, f32[200,768]{1,0:T(8,128)S(1)}, u32[]{:S(2)}, u32[]{:S(2)}) %collective-permute-start.40) | collective-permute-done | bytes 614432 | tf_op jit(solution)/shard_map/ppermute | solution.py:136
  439.2 2.8 maximum_add_fusion.1
  442.1 9.7 %collective-permute-done.37 = f32[200,768]{1,0:T(8,128)S(1)} collective-permute-done((f32[200,768]{1,0:T(8,128)S(1)}, f32[200,768]{1,0:T(8,128)S(1)}, u32[]{:S(2)}, u32[]{:S(2)}) %collective-permute-start.37) | collective-permute-done | bytes 614432 | tf_op jit(solution)/shard_map/ppermute | solution.py:136
  465.4 4.8 shard_map.193
  473.6 5.1 shard_map.192
  482.9 3.0 fusion.320
  493.8 4.4 fusion.67
  498.2 6.8 collective-permute-done.46
  506.5 11.2 %collective-permute-done.43 = f32[200,768]{1,0:T(8,128)} collective-permute-done((f32[200,768]{1,0:T(8,128)}, f32[200,768]{1,0:T(8,128)}, u32[]{:S(2)}, u32[]{:S(2)}) %collective-permute-start.43) | collective-permute-done | bytes 614432 | tf_op jit(solution)/shard_map/ppermute | solution.py:136
  520.7 3.4 fusion.63
  530.3 3.3 fusion.308
  540.5 6.3 copy.206
  559.3 3.8 reduce-scatter.19.cloned.1.call-done
  564.5 72.8 %reduce-scatter.13.cloned.1.call-done = f32[96,896]{1,0:T(8,128)} async-done(((f32[768,896]{1,0:T(8,128)}), f32[96,896]{1,0:T(8,128)}) %reduce-scatter.13.cloned.1.call-update) | async-done | bytes 344080
  643.9 91.8 %reduce-scatter.17.cloned.1.call-done = f32[96,1536]{1,0:T(8,128)} async-done(((f32[768,1536]{1,0:T(8,128)}), f32[96,1536]{1,0:T(8,128)}) %reduce-scatter.17.cloned.1.call-update) | async-done | bytes 589840
  (684 shorter events, 240.4 us)
Async XLA Ops:
  7.2 51.6 %all-gather.5.cloned.1.call-start = ((), (), s32[]{:S(2)}) async-start(), calls=%async_computation.4 | async-start | bytes 1548288 | tf_op jit(solution)/shard_map/all_gather | solution.py:164
  13.6 98.6 %all-gather.7.cloned.1.call-start = ((), (), s32[]{:S(2)}) async-start(), calls=%async_computation.5 | async-start | bytes 2654208 | tf_op jit(solution)/shard_map/all_gather | solution.py:165
  16.8 139.1 %all-gather.9.cloned.1.call-start = ((), (), s32[]{:S(2)}) async-start(), calls=%async_computation.6 | async-start | bytes 1548288 | tf_op jit(solution)/shard_map/all_gather | solution.py:164
  68.6 7.0 collective-permute-start.12
  75.7 16.7 %collective-permute-start.13 = (f32[200,768]{1,0:T(8,128)S(1)}, f32[200,768]{1,0:T(8,128)S(1)}, u32[]{:S(2)}, u32[]{:S(2)}) collective-permute-start(f32[200,768]{1,0:T(8,128)S(1)} %slice_add_fusion.11), channel_id=1, source_target_pairs={{0,2},{2,0},{1,3},{3,1},{4,6},{6,4},{5,7},{7,5},{8,10},{10,8},{9,1... | collective-permute-start | bytes 1843208 | tf_op jit(solution)/shard_map/ppermute | solution.py:136
  77.7 27.5 %collective-permute-start.1 = (f32[200,768]{1,0:T(8,128)S(1)}, f32[200,768]{1,0:T(8,128)S(1)}, u32[]{:S(2)}, u32[]{:S(2)}) collective-permute-start(f32[200,768]{1,0:T(8,128)S(1)} %slice_add_fusion.15), channel_id=1, source_target_pairs={{0,2},{2,0},{1,3},{3,1},{4,6},{6,4},{5,7},{7,5},{8,10},{10,8},{9,1... | collective-permute-start | bytes 1843208 | tf_op jit(solution)/shard_map/ppermute | solution.py:136
  92.5 14.3 %collective-permute-start.14 = (f32[200,768]{1,0:T(8,128)S(1)}, f32[200,768]{1,0:T(8,128)S(1)}, u32[]{:S(2)}, u32[]{:S(2)}) collective-permute-start(f32[200,768]{1,0:T(8,128)S(1)} %add.1181), channel_id=1, source_target_pairs={{0,1},{1,0},{2,3},{3,2},{4,5},{5,4},{6,7},{7,6},{8,9},{9,8},{10,11... | collective-permute-start | bytes 1843208 | tf_op jit(solution)/shard_map/ppermute | solution.py:137
  106.2 112.3 %all-gather.11.cloned.1.call-start = ((), (), s32[]{:S(2)}) async-start(), calls=%async_computation.7 | async-start | bytes 2654208 | tf_op jit(solution)/shard_map/all_gather | solution.py:165
  123.4 16.8 %collective-permute-start.16 = (f32[200,768]{1,0:T(8,128)S(1)}, f32[200,768]{1,0:T(8,128)S(1)}, u32[]{:S(2)}, u32[]{:S(2)}) collective-permute-start(f32[200,768]{1,0:T(8,128)S(1)} %slice_add_fusion.10), channel_id=1, source_target_pairs={{0,2},{2,0},{1,3},{3,1},{4,6},{6,4},{5,7},{7,5},{8,10},{10,8},{9,1... | collective-permute-start | bytes 1843208 | tf_op jit(solution)/shard_map/ppermute | solution.py:136
  125.1 27.3 %collective-permute-start.4 = (f32[200,768]{1,0:T(8,128)S(1)}, f32[200,768]{1,0:T(8,128)S(1)}, u32[]{:S(2)}, u32[]{:S(2)}) collective-permute-start(f32[200,768]{1,0:T(8,128)S(1)} %slice_add_fusion.14), channel_id=1, source_target_pairs={{0,2},{2,0},{1,3},{3,1},{4,6},{6,4},{5,7},{7,5},{8,10},{10,8},{9,1... | collective-permute-start | bytes 1843208 | tf_op jit(solution)/shard_map/ppermute | solution.py:136
  141.1 22.2 %collective-permute-start.17 = (f32[200,768]{1,0:T(8,128)}, f32[200,768]{1,0:T(8,128)}, u32[]{:S(2)}, u32[]{:S(2)}) collective-permute-start(f32[200,768]{1,0:T(8,128)} %add.1191), channel_id=1, source_target_pairs={{0,1},{1,0},{2,3},{3,2},{4,5},{5,4},{6,7},{7,6},{8,9},{9,8},{10,11... | collective-permute-start | bytes 1843208 | tf_op jit(solution)/shard_map/ppermute | solution.py:137
  153.3 10.0 %collective-permute-start.5 = (f32[200,768]{1,0:T(8,128)}, f32[200,768]{1,0:T(8,128)}, u32[]{:S(2)}, u32[]{:S(2)}) collective-permute-start(f32[200,768]{1,0:T(8,128)} %add.1143), channel_id=1, source_target_pairs={{0,1},{1,0},{2,3},{3,2},{4,5},{5,4},{6,7},{7,6},{8,9},{9,8},{10,11... | collective-permute-start | bytes 1843208 | tf_op jit(solution)/shard_map/ppermute | solution.py:137
  154.1 402.6 %reduce-scatter.15.cloned.1.call-start = ((), (), s32[]{:S(2)}) async-start(), calls=%async_computation.9 | async-start | bytes 3096576
  171.8 16.2 %collective-permute-start.18 = (f32[200,768]{1,0:T(8,128)S(1)}, f32[200,768]{1,0:T(8,128)S(1)}, u32[]{:S(2)}, u32[]{:S(2)}) collective-permute-start(f32[200,768]{1,0:T(8,128)S(1)} %slice.579), channel_id=1, source_target_pairs={{0,1},{1,0},{2,3},{3,2},{4,5},{5,4},{6,7},{7,6},{8,9},{9,8},{10,11... | collective-permute-start | bytes 1843208 | tf_op jit(solution)/shard_map/ppermute | solution.py:135
  188.2 16.9 %collective-permute-start.19 = (f32[200,768]{1,0:T(8,128)S(1)}, f32[200,768]{1,0:T(8,128)}, u32[]{:S(2)}, u32[]{:S(2)}) collective-permute-start(f32[200,768]{1,0:T(8,128)S(1)} %slice_add_fusion.9), channel_id=1, source_target_pairs={{0,2},{2,0},{1,3},{3,1},{4,6},{6,4},{5,7},{7,5},{8,10},{10,8},{9,1... | collective-permute-start | bytes 1843208 | tf_op jit(solution)/shard_map/ppermute | solution.py:136
  189.8 27.5 %collective-permute-start.7 = (f32[200,768]{1,0:T(8,128)S(1)}, f32[200,768]{1,0:T(8,128)}, u32[]{:S(2)}, u32[]{:S(2)}) collective-permute-start(f32[200,768]{1,0:T(8,128)S(1)} %slice_add_fusion.13), channel_id=1, source_target_pairs={{0,2},{2,0},{1,3},{3,1},{4,6},{6,4},{5,7},{7,5},{8,10},{10,8},{9,1... | collective-permute-start | bytes 1843208 | tf_op jit(solution)/shard_map/ppermute | solution.py:136
  207.1 14.8 %collective-permute-start.20 = (f32[200,768]{1,0:T(8,128)}, f32[200,768]{1,0:T(8,128)}, u32[]{:S(2)}, u32[]{:S(2)}) collective-permute-start(f32[200,768]{1,0:T(8,128)} %add.1199), channel_id=1, source_target_pairs={{0,1},{1,0},{2,3},{3,2},{4,5},{5,4},{6,7},{7,6},{8,9},{9,8},{10,11... | collective-permute-start | bytes 1843208 | tf_op jit(solution)/shard_map/ppermute | solution.py:137
  228.3 23.0 %collective-permute-start.9 = (f32[200,768]{1,0:T(8,128)S(1)}, f32[200,768]{1,0:T(8,128)S(1)}, u32[]{:S(2)}, u32[]{:S(2)}) collective-permute-start(f32[200,768]{1,0:T(8,128)S(1)} %slice.570), channel_id=1, source_target_pairs={{0,1},{1,0},{2,3},{3,2},{4,5},{5,4},{6,7},{7,6},{8,9},{9,8},{10,11... | collective-permute-start | bytes 1843208 | tf_op jit(solution)/shard_map/ppermute | solution.py:135
  232.0 20.0 %collective-permute-start.21 = (f32[200,768]{1,0:T(8,128)S(1)}, f32[200,768]{1,0:T(8,128)S(1)}, u32[]{:S(2)}, u32[]{:S(2)}) collective-permute-start(f32[200,768]{1,0:T(8,128)S(1)} %slice.581), channel_id=1, source_target_pairs={{0,1},{1,0},{2,3},{3,2},{4,5},{5,4},{6,7},{7,6},{8,9},{9,8},{10,11... | collective-permute-start | bytes 1843208 | tf_op jit(solution)/shard_map/ppermute | solution.py:135
  242.1 7.2 collective-permute-start.27
  248.8 5.6 collective-permute-start.24
  249.4 17.2 %collective-permute-start.28 = (f32[200,768]{1,0:T(8,128)S(1)}, f32[200,768]{1,0:T(8,128)S(1)}, u32[]{:S(2)}, u32[]{:S(2)}) collective-permute-start(f32[200,768]{1,0:T(8,128)S(1)} %slice_add_fusion.6), channel_id=1, source_target_pairs={{0,2},{2,0},{1,3},{3,1},{4,6},{6,4},{5,7},{7,5},{8,10},{10,8},{9,1... | collective-permute-start | bytes 1843208 | tf_op jit(solution)/shard_map/ppermute | solution.py:136
  251.4 28.5 %collective-permute-start.10 = (f32[200,768]{1,0:T(8,128)S(1)}, f32[200,768]{1,0:T(8,128)}, u32[]{:S(2)}, u32[]{:S(2)}) collective-permute-start(f32[200,768]{1,0:T(8,128)S(1)} %slice_add_fusion.12), channel_id=1, source_target_pairs={{0,2},{2,0},{1,3},{3,1},{4,6},{6,4},{5,7},{7,5},{8,10},{10,8},{9,1... | collective-permute-start | bytes 1843208 | tf_op jit(solution)/shard_map/ppermute | solution.py:136
  252.9 40.1 %collective-permute-start.22 = (f32[200,768]{1,0:T(8,128)}, f32[200,768]{1,0:T(8,128)}, u32[]{:S(2)}, u32[]{:S(2)}) collective-permute-start(f32[200,768]{1,0:T(8,128)} %slice_add_fusion.8), channel_id=1, source_target_pairs={{0,2},{2,0},{1,3},{3,1},{4,6},{6,4},{5,7},{7,5},{8,10},{10,8},{9,1... | collective-permute-start | bytes 1843208 | tf_op jit(solution)/shard_map/ppermute | solution.py:136
  254.5 50.8 %collective-permute-start.25 = (f32[200,768]{1,0:T(8,128)S(1)}, f32[200,768]{1,0:T(8,128)}, u32[]{:S(2)}, u32[]{:S(2)}) collective-permute-start(f32[200,768]{1,0:T(8,128)S(1)} %slice_add_fusion.7), channel_id=1, source_target_pairs={{0,2},{2,0},{1,3},{3,1},{4,6},{6,4},{5,7},{7,5},{8,10},{10,8},{9,1... | collective-permute-start | bytes 1843208 | tf_op jit(solution)/shard_map/ppermute | solution.py:136
  266.7 39.8 %collective-permute-start.29 = (f32[200,768]{1,0:T(8,128)S(1)}, f32[200,768]{1,0:T(8,128)S(1)}, u32[]{:S(2)}, u32[]{:S(2)}) collective-permute-start(f32[200,768]{1,0:T(8,128)S(1)} %get-tuple-element.143), channel_id=1, source_target_pairs={{0,1},{1,0},{2,3},{3,2},{4,5},{5,4},{6,7},{7,6},{8,9},{9,8},{10,11... | collective-permute-start | bytes 1843208 | tf_op jit(solution)/shard_map/ppermute | solution.py:137
  281.0 30.0 %collective-permute-start.11 = (f32[200,768]{1,0:T(8,128)S(1)}, f32[200,768]{1,0:T(8,128)S(1)}, u32[]{:S(2)}, u32[]{:S(2)}) collective-permute-start(f32[200,768]{1,0:T(8,128)S(1)} %add.1171), channel_id=1, source_target_pairs={{0,1},{1,0},{2,3},{3,2},{4,5},{5,4},{6,7},{7,6},{8,9},{9,8},{10,11... | collective-permute-start | bytes 1843208 | tf_op jit(solution)/shard_map/ppermute | solution.py:137
  294.3 12.9 %collective-permute-start.23 = (f32[200,768]{1,0:T(8,128)S(1)}, f32[200,768]{1,0:T(8,128)S(1)}, u32[]{:S(2)}, u32[]{:S(2)}) collective-permute-start(f32[200,768]{1,0:T(8,128)S(1)} %add.1209), channel_id=1, source_target_pairs={{0,1},{1,0},{2,3},{3,2},{4,5},{5,4},{6,7},{7,6},{8,9},{9,8},{10,11... | collective-permute-start | bytes 1843208 | tf_op jit(solution)/shard_map/ppermute | solution.py:137
  332.1 7.3 collective-permute-start.33
  335.9 7.0 collective-permute-start.30
  341.5 17.0 %collective-permute-start.34 = (f32[200,768]{1,0:T(8,128)}, f32[200,768]{1,0:T(8,128)}, u32[]{:S(2)}, u32[]{:S(2)}) collective-permute-start(f32[200,768]{1,0:T(8,128)} %slice_add_fusion.4), channel_id=1, source_target_pairs={{0,2},{2,0},{1,3},{3,1},{4,6},{6,4},{5,7},{7,5},{8,10},{10,8},{9,1... | collective-permute-start | bytes 1843208 | tf_op jit(solution)/shard_map/ppermute | solution.py:136
  344.9 26.1 %collective-permute-start.31 = (f32[200,768]{1,0:T(8,128)}, f32[200,768]{1,0:T(8,128)}, u32[]{:S(2)}, u32[]{:S(2)}) collective-permute-start(f32[200,768]{1,0:T(8,128)} %slice_add_fusion.5), channel_id=1, source_target_pairs={{0,2},{2,0},{1,3},{3,1},{4,6},{6,4},{5,7},{7,5},{8,10},{10,8},{9,1... | collective-permute-start | bytes 1843208 | tf_op jit(solution)/shard_map/ppermute | solution.py:136
  360.6 18.7 %collective-permute-start.35 = (f32[200,768]{1,0:T(8,128)}, f32[200,768]{1,0:T(8,128)}, u32[]{:S(2)}, u32[]{:S(2)}) collective-permute-start(f32[200,768]{1,0:T(8,128)} %get-tuple-element.147), channel_id=1, source_target_pairs={{0,1},{1,0},{2,3},{3,2},{4,5},{5,4},{6,7},{7,6},{8,9},{9,8},{10,11... | collective-permute-start | bytes 1843208 | tf_op jit(solution)/shard_map/ppermute | solution.py:137
  373.2 7.4 collective-permute-start.32
  395.2 167.9 %reduce-scatter.19.cloned.1.call-start = ((), (), s32[]{:S(2)}) async-start(), calls=%async_computation.11 | async-start | bytes 5308416
  401.4 235.9 %reduce-scatter.13.cloned.1.call-start = ((), (), s32[]{:S(2)}) async-start(), calls=%async_computation.8 | async-start | bytes 3096576
  410.6 15.8 %collective-permute-start.36 = (f32[200,768]{1,0:T(8,128)S(1)}, f32[200,768]{1,0:T(8,128)S(1)}, u32[]{:S(2)}, u32[]{:S(2)}) collective-permute-start(f32[200,768]{1,0:T(8,128)S(1)} %slice.593), channel_id=1, source_target_pairs={{0,1},{1,0},{2,3},{3,2},{4,5},{5,4},{6,7},{7,6},{8,9},{9,8},{10,11... | collective-permute-start | bytes 1843208 | tf_op jit(solution)/shard_map/ppermute | solution.py:135
  415.5 6.7 collective-permute-start.39
  422.3 16.7 %collective-permute-start.40 = (f32[200,768]{1,0:T(8,128)S(1)}, f32[200,768]{1,0:T(8,128)S(1)}, u32[]{:S(2)}, u32[]{:S(2)}) collective-permute-start(f32[200,768]{1,0:T(8,128)S(1)} %slice_add_fusion.2), channel_id=1, source_target_pairs={{0,2},{2,0},{1,3},{3,1},{4,6},{6,4},{5,7},{7,5},{8,10},{10,8},{9,1... | collective-permute-start | bytes 1843208 | tf_op jit(solution)/shard_map/ppermute | solution.py:136
  426.5 25.3 %collective-permute-start.37 = (f32[200,768]{1,0:T(8,128)S(1)}, f32[200,768]{1,0:T(8,128)S(1)}, u32[]{:S(2)}, u32[]{:S(2)}) collective-permute-start(f32[200,768]{1,0:T(8,128)S(1)} %slice_add_fusion.3), channel_id=1, source_target_pairs={{0,2},{2,0},{1,3},{3,1},{4,6},{6,4},{5,7},{7,5},{8,10},{10,8},{9,1... | collective-permute-start | bytes 1843208 | tf_op jit(solution)/shard_map/ppermute | solution.py:136
  439.2 13.9 %collective-permute-start.41 = (f32[200,768]{1,0:T(8,128)S(1)}, f32[200,768]{1,0:T(8,128)S(1)}, u32[]{:S(2)}, u32[]{:S(2)}) collective-permute-start(f32[200,768]{1,0:T(8,128)S(1)} %get-tuple-element.127), channel_id=1, source_target_pairs={{0,1},{1,0},{2,3},{3,2},{4,5},{5,4},{6,7},{7,6},{8,9},{9,8},{10,11... | collective-permute-start | bytes 1843208 | tf_op jit(solution)/shard_map/ppermute | solution.py:137
  473.0 13.0 %collective-permute-start.45 = (f32[200,768]{1,0:T(8,128)}, f32[200,768]{1,0:T(8,128)}, u32[]{:S(2)}, u32[]{:S(2)}) collective-permute-start(f32[200,768]{1,0:T(8,128)} %slice.601), channel_id=1, source_target_pairs={{0,1},{1,0},{2,3},{3,2},{4,5},{5,4},{6,7},{7,6},{8,9},{9,8},{10,11... | collective-permute-start | bytes 1843208 | tf_op jit(solution)/shard_map/ppermute | solution.py:135
  482.1 7.5 collective-permute-start.42
  488.0 17.0 %collective-permute-start.46 = (f32[200,768]{1,0:T(8,128)}, f32[200,768]{1,0:T(8,128)}, u32[]{:S(2)}, u32[]{:S(2)}) collective-permute-start(f32[200,768]{1,0:T(8,128)} %slice_add_fusion), channel_id=1, source_target_pairs={{0,2},{2,0},{1,3},{3,1},{4,6},{6,4},{5,7},{7,5},{8,10},{10,8},{9,1... | collective-permute-start | bytes 1843208 | tf_op jit(solution)/shard_map/ppermute | solution.py:136
  490.4 27.2 %collective-permute-start.43 = (f32[200,768]{1,0:T(8,128)}, f32[200,768]{1,0:T(8,128)}, u32[]{:S(2)}, u32[]{:S(2)}) collective-permute-start(f32[200,768]{1,0:T(8,128)} %slice_add_fusion.1), channel_id=1, source_target_pairs={{0,2},{2,0},{1,3},{3,1},{4,6},{6,4},{5,7},{7,5},{8,10},{10,8},{9,1... | collective-permute-start | bytes 1843208 | tf_op jit(solution)/shard_map/ppermute | solution.py:136
  506.4 19.5 %collective-permute-start.47 = (f32[200,768]{1,0:T(8,128)S(1)}, f32[200,768]{1,0:T(8,128)}, u32[]{:S(2)}, u32[]{:S(2)}) collective-permute-start(f32[200,768]{1,0:T(8,128)S(1)} %get-tuple-element.131), channel_id=1, source_target_pairs={{0,1},{1,0},{2,3},{3,2},{4,5},{5,4},{6,7},{7,6},{8,9},{9,8},{10,11... | collective-permute-start | bytes 1843208 | tf_op jit(solution)/shard_map/ppermute | solution.py:137
  519.8 7.3 collective-permute-start.44
  540.4 195.3 %reduce-scatter.17.cloned.1.call-start = ((), (), s32[]{:S(2)}) async-start(), calls=%async_computation.10 | async-start | bytes 5308416
  (119 other events, 738.5 us)
Sparse Core Ops, SparseCore 0:
  13.7 44.9 all-gather.4
  61.5 50.6 all-gather.6
  114.9 40.8 all-gather.8
  158.4 50.5 all-gather.10
  395.3 69.8 reduce-scatter.14
  468.7 94.3 reduce-scatter.18
  566.6 70.6 reduce-scatter.12
  641.0 94.6 reduce-scatter.16

commit v3 on v2

--- a/solution.py
+++ b/solution.py
@@ -322,7 +322,8 @@
         columns = -(-flat.shape[1] // depth)
         flat = jnp.pad(flat, ((0, 0), (0, columns * depth - flat.shape[1])))
         flat = flat.reshape(n, columns, depth).transpose(1, 0, 2).reshape(columns, width)
-        small = jnp.concatenate([six, flat]).T
+        filler = jnp.tile(feed_total[:, :1], (n, 1))
+        small = jnp.concatenate([jnp.concatenate([six, flat]).T, filler], axis=1)
         small = jnp.pad(small, ((0, 0), (0, 128 - small.shape[1])))
         attention_total = lax.psum_scatter(
             jnp.concatenate([both[0][1] + both[1][1], small], axis=1),

time: 757 us -> 726 us (0.959)
  waiting for transfers between devices: 382 us -> 369 us
  Pallas kernels: 41.8 us -> 33.1 us
    unnamed x12, waiting for transfers between devices: 169 us -> 146 us
    ppermute x16, waiting for transfers between devices: 170 us -> 180 us  [tensor_sum(): mine = mine + lax.ppermute(mine, 'tensor', chip_pairs)]
    pallas_call x8, Pallas kernels: 41.8 us -> 33.1 us  [attention_call(): pl.pallas_call(lambda *refs: kernel(heads, head_dim, tokens, *refs), grid...]
    unnamed x237 -> x227, local copies, waits for them, and re-layouts: 51.1 us -> 49.8 us
  transfers between devices with their start and end apart: 56 -> 56, of which waited for: 27 -> 27; matrix products, arithmetic and copies ran while one was open for 29% -> 31% of each run, Pallas kernels for 4% -> 3%
where the time goes in v3:
time: 726 us; the launch traced here: 716 us
  waiting for transfers between devices  369 us (51%)
  matrix products  97.7 us (13%)
  other arithmetic  93.1 us (13%)
  local copies, waits for them, and re-layouts  77.6 us (11%)
  Pallas kernels  33.1 us (5%)
  starting transfers between devices  27.7 us (4%)
  between operations  17.7 us (2%)
    ppermute x16, waiting for transfers between devices, tensor_sum(): mine = mine + lax.ppermute(mine, 'tensor', chip_pairs)  180 us
    unnamed x12, waiting for transfers between devices  146 us
    unnamed x227, local copies, waits for them, and re-layouts  49.8 us
    dot_general x16, matrix products, cross(): lax.dot_general(a, b, (((0,), (0,)), ((), ())), precision=high, preferred...  41.3 us
    all_gather x2, waiting for transfers between devices, gather_weights(): attention = lax.all_gather(attention, 'dp', axis=0, tiled=True)  37.8 us
    pallas_call x8, Pallas kernels, attention_call(): pl.pallas_call(lambda *refs: kernel(heads, head_dim, tokens, *refs), grid...  33.1 us
    dot_general x32, matrix products, weight_product(): lax.dot_general(rest, w, dims, preferred_element_type=f32)  29.5 us
    dot_general x32, matrix products, weight_product(): lax.dot_general(top.astype(bf16), w, dims, preferred_element_type=f32)  26.9 us
  transfers between devices with their start and end apart: 56, of which 27 were waited for; matrix products, arithmetic and copies ran while one was open for 31% of the time, Pallas kernels for 3%

profile of v3, /device:TPU:0, one launch (start us, length us, event | category | flops | bytes accessed | tf_op | source)
XLA Modules:
  0.0 715.9 jit_solution(11478843338947029461)
XLA Ops:
  22.5 37.7 %all-gather.5.cloned.1.call-done = bf16[768,896]{1,0:T(8,128)(2,1)} async-done(((bf16[96,896]{1,0:T(8,128)(2,1)}), bf16[768,896]{1,0:T(8,128)(2,1)}) %all-gather.5.cloned.1.call-update) | async-done | bytes 1376272 | tf_op jit(solution)/shard_map/all_gather | solution.py:164
  65.8 3.3 shard_map.188.refs_2_
  72.7 3.3 shard_map.186.refs_2_
  80.7 13.1 %collective-permute-done.13 = f32[200,768]{1,0:T(8,128)S(1)} collective-permute-done((f32[200,768]{1,0:T(8,128)S(1)}, f32[200,768]{1,0:T(8,128)S(1)}, u32[]{:S(2)}, u32[]{:S(2)}) %collective-permute-start.13) | collective-permute-done | bytes 614432 | tf_op jit(solution)/shard_map/ppermute | solution.py:136
  94.0 12.6 %collective-permute-done.1 = f32[200,768]{1,0:T(8,128)S(1)} collective-permute-done((f32[200,768]{1,0:T(8,128)S(1)}, f32[200,768]{1,0:T(8,128)S(1)}, u32[]{:S(2)}, u32[]{:S(2)}) %collective-permute-start.1) | collective-permute-done | bytes 614432 | tf_op jit(solution)/shard_map/ppermute | solution.py:136
  109.3 3.5 fusion.49
  131.6 13.1 %collective-permute-done.16 = f32[200,768]{1,0:T(8,128)S(1)} collective-permute-done((f32[200,768]{1,0:T(8,128)S(1)}, f32[200,768]{1,0:T(8,128)S(1)}, u32[]{:S(2)}, u32[]{:S(2)}) %collective-permute-start.16) | collective-permute-done | bytes 614432 | tf_op jit(solution)/shard_map/ppermute | solution.py:136
  144.9 12.5 %collective-permute-done.4 = f32[200,768]{1,0:T(8,128)S(1)} collective-permute-done((f32[200,768]{1,0:T(8,128)S(1)}, f32[200,768]{1,0:T(8,128)S(1)}, u32[]{:S(2)}, u32[]{:S(2)}) %collective-permute-start.4) | collective-permute-done | bytes 614432 | tf_op jit(solution)/shard_map/ppermute | solution.py:136
  166.4 3.3 shard_map.189.refs_2_
  173.2 3.5 shard_map.187.refs_2_
  184.9 10.4 %collective-permute-done.19 = f32[200,768]{1,0:T(8,128)} collective-permute-done((f32[200,768]{1,0:T(8,128)S(1)}, f32[200,768]{1,0:T(8,128)}, u32[]{:S(2)}, u32[]{:S(2)}) %collective-permute-start.19) | collective-permute-done | bytes 614432 | tf_op jit(solution)/shard_map/ppermute | solution.py:136
  197.4 10.7 %collective-permute-done.7 = f32[200,768]{1,0:T(8,128)} collective-permute-done((f32[200,768]{1,0:T(8,128)S(1)}, f32[200,768]{1,0:T(8,128)}, u32[]{:S(2)}, u32[]{:S(2)}) %collective-permute-start.7) | collective-permute-done | bytes 614432 | tf_op jit(solution)/shard_map/ppermute | solution.py:136
  225.8 3.1 fusion.66
  229.8 2.7 fusion.70
  238.5 2.6 fusion.269
  246.9 11.4 %collective-permute-done.28 = f32[200,768]{1,0:T(8,128)S(1)} collective-permute-done((f32[200,768]{1,0:T(8,128)S(1)}, f32[200,768]{1,0:T(8,128)S(1)}, u32[]{:S(2)}, u32[]{:S(2)}) %collective-permute-start.28) | collective-permute-done | bytes 614432 | tf_op jit(solution)/shard_map/ppermute | solution.py:136
  258.4 2.7 maximum_add_fusion
  261.2 10.4 %collective-permute-done.10 = f32[200,768]{1,0:T(8,128)} collective-permute-done((f32[200,768]{1,0:T(8,128)S(1)}, f32[200,768]{1,0:T(8,128)}, u32[]{:S(2)}, u32[]{:S(2)}) %collective-permute-start.10) | collective-permute-done | bytes 614432 | tf_op jit(solution)/shard_map/ppermute | solution.py:136
  272.8 11.9 %collective-permute-done.22 = f32[200,768]{1,0:T(8,128)} collective-permute-done((f32[200,768]{1,0:T(8,128)}, f32[200,768]{1,0:T(8,128)}, u32[]{:S(2)}, u32[]{:S(2)}) %collective-permute-start.22) | collective-permute-done | bytes 614432 | tf_op jit(solution)/shard_map/ppermute | solution.py:136
  286.1 11.4 %collective-permute-done.25 = f32[200,768]{1,0:T(8,128)} collective-permute-done((f32[200,768]{1,0:T(8,128)S(1)}, f32[200,768]{1,0:T(8,128)}, u32[]{:S(2)}, u32[]{:S(2)}) %collective-permute-start.25) | collective-permute-done | bytes 614432 | tf_op jit(solution)/shard_map/ppermute | solution.py:136
  307.8 4.9 shard_map.190
  317.0 4.9 shard_map.191
  328.7 13.5 %collective-permute-done.34 = f32[200,768]{1,0:T(8,128)S(1)} collective-permute-done((f32[200,768]{1,0:T(8,128)S(1)}, f32[200,768]{1,0:T(8,128)S(1)}, u32[]{:S(2)}, u32[]{:S(2)}) %collective-permute-start.34) | collective-permute-done | bytes 614432 | tf_op jit(solution)/shard_map/ppermute | solution.py:136
  343.2 11.4 %collective-permute-done.31 = f32[200,768]{1,0:T(8,128)S(1)} collective-permute-done((f32[200,768]{1,0:T(8,128)S(1)}, f32[200,768]{1,0:T(8,128)S(1)}, u32[]{:S(2)}, u32[]{:S(2)}) %collective-permute-start.31) | collective-permute-done | bytes 614432 | tf_op jit(solution)/shard_map/ppermute | solution.py:136
  355.5 6.1 copy.206
  361.7 3.5 multiply_reduce_fusion.2
  365.6 3.2 fusion.282
  377.9 2.7 fusion.64
  383.2 2.9 fusion.68
  392.3 10.7 %collective-permute-done.40 = f32[200,768]{1,0:T(8,128)S(1)} collective-permute-done((f32[200,768]{1,0:T(8,128)S(1)}, f32[200,768]{1,0:T(8,128)S(1)}, u32[]{:S(2)}, u32[]{:S(2)}) %collective-permute-start.40) | collective-permute-done | bytes 614432 | tf_op jit(solution)/shard_map/ppermute | solution.py:136
  403.1 2.7 maximum_add_fusion.1
  405.9 9.4 %collective-permute-done.37 = f32[200,768]{1,0:T(8,128)} collective-permute-done((f32[200,768]{1,0:T(8,128)}, f32[200,768]{1,0:T(8,128)}, u32[]{:S(2)}, u32[]{:S(2)}) %collective-permute-start.37) | collective-permute-done | bytes 614432 | tf_op jit(solution)/shard_map/ppermute | solution.py:136
  422.7 6.1 copy.202
  452.9 5.1 shard_map.193
  461.3 4.9 shard_map.192
  469.0 3.4 pad_maximum_fusion.1
  472.3 3.4 copy.208
  481.2 3.0 fusion.320
  492.3 4.4 fusion.67
  496.7 6.8 collective-permute-done.46
  504.9 11.2 %collective-permute-done.43 = f32[200,768]{1,0:T(8,128)} collective-permute-done((f32[200,768]{1,0:T(8,128)}, f32[200,768]{1,0:T(8,128)}, u32[]{:S(2)}, u32[]{:S(2)}) %collective-permute-start.43) | collective-permute-done | bytes 614432 | tf_op jit(solution)/shard_map/ppermute | solution.py:136
  518.8 3.4 fusion.63
  528.2 3.2 fusion.308
  531.5 2.9 fusion.307
  534.5 20.0 %reduce-scatter.13.cloned.1.call-done = f32[96,1536]{1,0:T(8,128)} async-done(((f32[768,1536]{1,0:T(8,128)}), f32[96,1536]{1,0:T(8,128)}) %reduce-scatter.13.cloned.1.call-update) | async-done | bytes 589840
  557.2 3.5 copy.204
  574.3 54.4 %reduce-scatter.19.cloned.1.call-done = f32[96,896]{1,0:T(8,128)} async-done(((f32[768,896]{1,0:T(8,128)}), f32[96,896]{1,0:T(8,128)}) %reduce-scatter.19.cloned.1.call-update) | async-done | bytes 344080
  631.2 71.2 %reduce-scatter.15.cloned.1.call-done = f32[96,896]{1,0:T(8,128)} async-done(((f32[768,896]{1,0:T(8,128)}), f32[96,896]{1,0:T(8,128)}) %reduce-scatter.15.cloned.1.call-update) | async-done | bytes 344080
  (681 shorter events, 232.4 us)
Async XLA Ops:
  7.2 53.1 %all-gather.5.cloned.1.call-start = ((), (), s32[]{:S(2)}) async-start(), calls=%async_computation.4 | async-start | bytes 1548288 | tf_op jit(solution)/shard_map/all_gather | solution.py:164
  14.9 101.4 %all-gather.7.cloned.1.call-start = ((), (), s32[]{:S(2)}) async-start(), calls=%async_computation.5 | async-start | bytes 2654208 | tf_op jit(solution)/shard_map/all_gather | solution.py:165
  17.1 142.2 %all-gather.9.cloned.1.call-start = ((), (), s32[]{:S(2)}) async-start(), calls=%async_computation.6 | async-start | bytes 1548288 | tf_op jit(solution)/shard_map/all_gather | solution.py:164
  70.1 7.0 collective-permute-start.12
  77.1 16.7 %collective-permute-start.13 = (f32[200,768]{1,0:T(8,128)S(1)}, f32[200,768]{1,0:T(8,128)S(1)}, u32[]{:S(2)}, u32[]{:S(2)}) collective-permute-start(f32[200,768]{1,0:T(8,128)S(1)} %slice_add_fusion.11), channel_id=1, source_target_pairs={{0,2},{2,0},{1,3},{3,1},{4,6},{6,4},{5,7},{7,5},{8,10},{10,8},{9,1... | collective-permute-start | bytes 1843208 | tf_op jit(solution)/shard_map/ppermute | solution.py:136
  79.1 27.5 %collective-permute-start.1 = (f32[200,768]{1,0:T(8,128)S(1)}, f32[200,768]{1,0:T(8,128)S(1)}, u32[]{:S(2)}, u32[]{:S(2)}) collective-permute-start(f32[200,768]{1,0:T(8,128)S(1)} %slice_add_fusion.15), channel_id=1, source_target_pairs={{0,2},{2,0},{1,3},{3,1},{4,6},{6,4},{5,7},{7,5},{8,10},{10,8},{9,1... | collective-permute-start | bytes 1843208 | tf_op jit(solution)/shard_map/ppermute | solution.py:136
  94.0 14.5 %collective-permute-start.14 = (f32[200,768]{1,0:T(8,128)S(1)}, f32[200,768]{1,0:T(8,128)S(1)}, u32[]{:S(2)}, u32[]{:S(2)}) collective-permute-start(f32[200,768]{1,0:T(8,128)S(1)} %add.1181), channel_id=1, source_target_pairs={{0,1},{1,0},{2,3},{3,2},{4,5},{5,4},{6,7},{7,6},{8,9},{9,8},{10,11... | collective-permute-start | bytes 1843208 | tf_op jit(solution)/shard_map/ppermute | solution.py:137
  107.7 102.8 %all-gather.11.cloned.1.call-start = ((), (), s32[]{:S(2)}) async-start(), calls=%async_computation.7 | async-start | bytes 2654208 | tf_op jit(solution)/shard_map/all_gather | solution.py:165
  122.8 5.1 collective-permute-start.15
  128.0 16.7 %collective-permute-start.16 = (f32[200,768]{1,0:T(8,128)S(1)}, f32[200,768]{1,0:T(8,128)S(1)}, u32[]{:S(2)}, u32[]{:S(2)}) collective-permute-start(f32[200,768]{1,0:T(8,128)S(1)} %slice_add_fusion.10), channel_id=1, source_target_pairs={{0,2},{2,0},{1,3},{3,1},{4,6},{6,4},{5,7},{7,5},{8,10},{10,8},{9,1... | collective-permute-start | bytes 1843208 | tf_op jit(solution)/shard_map/ppermute | solution.py:136
  130.0 27.4 %collective-permute-start.4 = (f32[200,768]{1,0:T(8,128)S(1)}, f32[200,768]{1,0:T(8,128)S(1)}, u32[]{:S(2)}, u32[]{:S(2)}) collective-permute-start(f32[200,768]{1,0:T(8,128)S(1)} %slice_add_fusion.14), channel_id=1, source_target_pairs={{0,2},{2,0},{1,3},{3,1},{4,6},{6,4},{5,7},{7,5},{8,10},{10,8},{9,1... | collective-permute-start | bytes 1843208 | tf_op jit(solution)/shard_map/ppermute | solution.py:136
  144.9 17.2 %collective-permute-start.17 = (f32[200,768]{1,0:T(8,128)S(1)}, f32[200,768]{1,0:T(8,128)}, u32[]{:S(2)}, u32[]{:S(2)}) collective-permute-start(f32[200,768]{1,0:T(8,128)S(1)} %add.1191), channel_id=1, source_target_pairs={{0,1},{1,0},{2,3},{3,2},{4,5},{5,4},{6,7},{7,6},{8,9},{9,8},{10,11... | collective-permute-start | bytes 1843208 | tf_op jit(solution)/shard_map/ppermute | solution.py:137
  158.4 3.6 collective-permute-start.5
  159.2 308.7 %reduce-scatter.17.cloned.1.call-start = ((), (), s32[]{:S(2)}) async-start(), calls=%async_computation.10 | async-start | bytes 5308416
  170.7 7.7 %collective-permute-start.18 = (f32[200,768]{1,0:T(8,128)S(1)}, f32[200,768]{1,0:T(8,128)S(1)}, u32[]{:S(2)}, u32[]{:S(2)}) collective-permute-start(f32[200,768]{1,0:T(8,128)S(1)} %slice.587), channel_id=1, source_target_pairs={{0,1},{1,0},{2,3},{3,2},{4,5},{5,4},{6,7},{7,6},{8,9},{9,8},{10,11... | collective-permute-start | bytes 1843208 | tf_op jit(solution)/shard_map/ppermute | solution.py:135
  178.5 16.8 %collective-permute-start.19 = (f32[200,768]{1,0:T(8,128)S(1)}, f32[200,768]{1,0:T(8,128)}, u32[]{:S(2)}, u32[]{:S(2)}) collective-permute-start(f32[200,768]{1,0:T(8,128)S(1)} %slice_add_fusion.9), channel_id=1, source_target_pairs={{0,2},{2,0},{1,3},{3,1},{4,6},{6,4},{5,7},{7,5},{8,10},{10,8},{9,1... | collective-permute-start | bytes 1843208 | tf_op jit(solution)/shard_map/ppermute | solution.py:136
  180.2 27.9 %collective-permute-start.7 = (f32[200,768]{1,0:T(8,128)S(1)}, f32[200,768]{1,0:T(8,128)}, u32[]{:S(2)}, u32[]{:S(2)}) collective-permute-start(f32[200,768]{1,0:T(8,128)S(1)} %slice_add_fusion.13), channel_id=1, source_target_pairs={{0,2},{2,0},{1,3},{3,1},{4,6},{6,4},{5,7},{7,5},{8,10},{10,8},{9,1... | collective-permute-start | bytes 1843208 | tf_op jit(solution)/shard_map/ppermute | solution.py:136
  197.4 16.5 %collective-permute-start.20 = (f32[200,768]{1,0:T(8,128)}, f32[200,768]{1,0:T(8,128)}, u32[]{:S(2)}, u32[]{:S(2)}) collective-permute-start(f32[200,768]{1,0:T(8,128)} %add.1199), channel_id=1, source_target_pairs={{0,1},{1,0},{2,3},{3,2},{4,5},{5,4},{6,7},{7,6},{8,9},{9,8},{10,11... | collective-permute-start | bytes 1843208 | tf_op jit(solution)/shard_map/ppermute | solution.py:137
  209.3 4.7 collective-permute-start.8
  220.3 22.7 %collective-permute-start.9 = (f32[200,768]{1,0:T(8,128)S(1)}, f32[200,768]{1,0:T(8,128)S(1)}, u32[]{:S(2)}, u32[]{:S(2)}) collective-permute-start(f32[200,768]{1,0:T(8,128)S(1)} %slice.578), channel_id=1, source_target_pairs={{0,1},{1,0},{2,3},{3,2},{4,5},{5,4},{6,7},{7,6},{8,9},{9,8},{10,11... | collective-permute-start | bytes 1843208 | tf_op jit(solution)/shard_map/ppermute | solution.py:135
  223.6 20.2 %collective-permute-start.21 = (f32[200,768]{1,0:T(8,128)S(1)}, f32[200,768]{1,0:T(8,128)S(1)}, u32[]{:S(2)}, u32[]{:S(2)}) collective-permute-start(f32[200,768]{1,0:T(8,128)S(1)} %slice.589), channel_id=1, source_target_pairs={{0,1},{1,0},{2,3},{3,2},{4,5},{5,4},{6,7},{7,6},{8,9},{9,8},{10,11... | collective-permute-start | bytes 1843208 | tf_op jit(solution)/shard_map/ppermute | solution.py:135
  234.0 7.2 %collective-permute-start.27 = (f32[200,768]{1,0:T(8,128)S(1)}, f32[200,768]{1,0:T(8,128)S(1)}, u32[]{:S(2)}, u32[]{:S(2)}) collective-permute-start(f32[200,768]{1,0:T(8,128)S(1)} %slice.595), channel_id=1, source_target_pairs={{0,1},{1,0},{2,3},{3,2},{4,5},{5,4},{6,7},{7,6},{8,9},{9,8},{10,11... | collective-permute-start | bytes 1843208 | tf_op jit(solution)/shard_map/ppermute | solution.py:135
  241.2 5.0 collective-permute-start.24
  241.3 16.9 %collective-permute-start.28 = (f32[200,768]{1,0:T(8,128)S(1)}, f32[200,768]{1,0:T(8,128)S(1)}, u32[]{:S(2)}, u32[]{:S(2)}) collective-permute-start(f32[200,768]{1,0:T(8,128)S(1)} %slice_add_fusion.6), channel_id=1, source_target_pairs={{0,2},{2,0},{1,3},{3,1},{4,6},{6,4},{5,7},{7,5},{8,10},{10,8},{9,1... | collective-permute-start | bytes 1843208 | tf_op jit(solution)/shard_map/ppermute | solution.py:136
  243.2 28.3 %collective-permute-start.10 = (f32[200,768]{1,0:T(8,128)S(1)}, f32[200,768]{1,0:T(8,128)}, u32[]{:S(2)}, u32[]{:S(2)}) collective-permute-start(f32[200,768]{1,0:T(8,128)S(1)} %slice_add_fusion.12), channel_id=1, source_target_pairs={{0,2},{2,0},{1,3},{3,1},{4,6},{6,4},{5,7},{7,5},{8,10},{10,8},{9,1... | collective-permute-start | bytes 1843208 | tf_op jit(solution)/shard_map/ppermute | solution.py:136
  244.7 40.0 %collective-permute-start.22 = (f32[200,768]{1,0:T(8,128)}, f32[200,768]{1,0:T(8,128)}, u32[]{:S(2)}, u32[]{:S(2)}) collective-permute-start(f32[200,768]{1,0:T(8,128)} %slice_add_fusion.8), channel_id=1, source_target_pairs={{0,2},{2,0},{1,3},{3,1},{4,6},{6,4},{5,7},{7,5},{8,10},{10,8},{9,1... | collective-permute-start | bytes 1843208 | tf_op jit(solution)/shard_map/ppermute | solution.py:136
  246.2 51.2 %collective-permute-start.25 = (f32[200,768]{1,0:T(8,128)S(1)}, f32[200,768]{1,0:T(8,128)}, u32[]{:S(2)}, u32[]{:S(2)}) collective-permute-start(f32[200,768]{1,0:T(8,128)S(1)} %slice_add_fusion.7), channel_id=1, source_target_pairs={{0,2},{2,0},{1,3},{3,1},{4,6},{6,4},{5,7},{7,5},{8,10},{10,8},{9,1... | collective-permute-start | bytes 1843208 | tf_op jit(solution)/shard_map/ppermute | solution.py:136
  258.3 40.3 %collective-permute-start.29 = (f32[200,768]{1,0:T(8,128)S(1)}, f32[200,768]{1,0:T(8,128)S(1)}, u32[]{:S(2)}, u32[]{:S(2)}) collective-permute-start(f32[200,768]{1,0:T(8,128)S(1)} %get-tuple-element.143), channel_id=1, source_target_pairs={{0,1},{1,0},{2,3},{3,2},{4,5},{5,4},{6,7},{7,6},{8,9},{9,8},{10,11... | collective-permute-start | bytes 1843208 | tf_op jit(solution)/shard_map/ppermute | solution.py:137
  272.7 30.5 %collective-permute-start.11 = (f32[200,768]{1,0:T(8,128)S(1)}, f32[200,768]{1,0:T(8,128)S(1)}, u32[]{:S(2)}, u32[]{:S(2)}) collective-permute-start(f32[200,768]{1,0:T(8,128)S(1)} %add.1171), channel_id=1, source_target_pairs={{0,1},{1,0},{2,3},{3,2},{4,5},{5,4},{6,7},{7,6},{8,9},{9,8},{10,11... | collective-permute-start | bytes 1843208 | tf_op jit(solution)/shard_map/ppermute | solution.py:137
  286.0 13.4 %collective-permute-start.23 = (f32[200,768]{1,0:T(8,128)S(1)}, f32[200,768]{1,0:T(8,128)S(1)}, u32[]{:S(2)}, u32[]{:S(2)}) collective-permute-start(f32[200,768]{1,0:T(8,128)S(1)} %add.1209), channel_id=1, source_target_pairs={{0,1},{1,0},{2,3},{3,2},{4,5},{5,4},{6,7},{7,6},{8,9},{9,8},{10,11... | collective-permute-start | bytes 1843208 | tf_op jit(solution)/shard_map/ppermute | solution.py:137
  325.5 16.8 %collective-permute-start.34 = (f32[200,768]{1,0:T(8,128)S(1)}, f32[200,768]{1,0:T(8,128)S(1)}, u32[]{:S(2)}, u32[]{:S(2)}) collective-permute-start(f32[200,768]{1,0:T(8,128)S(1)} %slice_add_fusion.4), channel_id=1, source_target_pairs={{0,2},{2,0},{1,3},{3,1},{4,6},{6,4},{5,7},{7,5},{8,10},{10,8},{9,1... | collective-permute-start | bytes 1843208 | tf_op jit(solution)/shard_map/ppermute | solution.py:136
  327.2 27.4 %collective-permute-start.31 = (f32[200,768]{1,0:T(8,128)S(1)}, f32[200,768]{1,0:T(8,128)S(1)}, u32[]{:S(2)}, u32[]{:S(2)}) collective-permute-start(f32[200,768]{1,0:T(8,128)S(1)} %slice_add_fusion.5), channel_id=1, source_target_pairs={{0,2},{2,0},{1,3},{3,1},{4,6},{6,4},{5,7},{7,5},{8,10},{10,8},{9,1... | collective-permute-start | bytes 1843208 | tf_op jit(solution)/shard_map/ppermute | solution.py:136
  343.2 18.6 %collective-permute-start.35 = (f32[200,768]{1,0:T(8,128)}, f32[200,768]{1,0:T(8,128)}, u32[]{:S(2)}, u32[]{:S(2)}) collective-permute-start(f32[200,768]{1,0:T(8,128)} %get-tuple-element.147), channel_id=1, source_target_pairs={{0,1},{1,0},{2,3},{3,2},{4,5},{5,4},{6,7},{7,6},{8,9},{9,8},{10,11... | collective-permute-start | bytes 1843208 | tf_op jit(solution)/shard_map/ppermute | solution.py:137
  355.5 6.2 collective-permute-start.32
  361.6 192.9 %reduce-scatter.13.cloned.1.call-start = ((), (), s32[]{:S(2)}) async-start(), calls=%async_computation.8 | async-start | bytes 5308416
  372.4 17.8 %collective-permute-start.36 = (f32[200,768]{1,0:T(8,128)S(1)}, f32[200,768]{1,0:T(8,128)S(1)}, u32[]{:S(2)}, u32[]{:S(2)}) collective-permute-start(f32[200,768]{1,0:T(8,128)S(1)} %slice.601), channel_id=1, source_target_pairs={{0,1},{1,0},{2,3},{3,2},{4,5},{5,4},{6,7},{7,6},{8,9},{9,8},{10,11... | collective-permute-start | bytes 1843208 | tf_op jit(solution)/shard_map/ppermute | solution.py:135
  376.6 9.4 %collective-permute-start.39 = (f32[200,768]{1,0:T(8,128)S(1)}, f32[200,768]{1,0:T(8,128)S(1)}, u32[]{:S(2)}, u32[]{:S(2)}) collective-permute-start(f32[200,768]{1,0:T(8,128)S(1)} %slice.603), channel_id=1, source_target_pairs={{0,1},{1,0},{2,3},{3,2},{4,5},{5,4},{6,7},{7,6},{8,9},{9,8},{10,11... | collective-permute-start | bytes 1843208 | tf_op jit(solution)/shard_map/ppermute | solution.py:135
  386.1 16.8 %collective-permute-start.40 = (f32[200,768]{1,0:T(8,128)S(1)}, f32[200,768]{1,0:T(8,128)S(1)}, u32[]{:S(2)}, u32[]{:S(2)}) collective-permute-start(f32[200,768]{1,0:T(8,128)S(1)} %slice_add_fusion.2), channel_id=1, source_target_pairs={{0,2},{2,0},{1,3},{3,1},{4,6},{6,4},{5,7},{7,5},{8,10},{10,8},{9,1... | collective-permute-start | bytes 1843208 | tf_op jit(solution)/shard_map/ppermute | solution.py:136
  391.1 24.1 %collective-permute-start.37 = (f32[200,768]{1,0:T(8,128)}, f32[200,768]{1,0:T(8,128)}, u32[]{:S(2)}, u32[]{:S(2)}) collective-permute-start(f32[200,768]{1,0:T(8,128)} %slice_add_fusion.3), channel_id=1, source_target_pairs={{0,2},{2,0},{1,3},{3,1},{4,6},{6,4},{5,7},{7,5},{8,10},{10,8},{9,1... | collective-permute-start | bytes 1843208 | tf_op jit(solution)/shard_map/ppermute | solution.py:136
  403.1 13.6 %collective-permute-start.41 = (f32[200,768]{1,0:T(8,128)S(1)}, f32[200,768]{1,0:T(8,128)S(1)}, u32[]{:S(2)}, u32[]{:S(2)}) collective-permute-start(f32[200,768]{1,0:T(8,128)S(1)} %get-tuple-element.127), channel_id=1, source_target_pairs={{0,1},{1,0},{2,3},{3,2},{4,5},{5,4},{6,7},{7,6},{8,9},{9,8},{10,11... | collective-permute-start | bytes 1843208 | tf_op jit(solution)/shard_map/ppermute | solution.py:137
  428.8 199.8 %reduce-scatter.19.cloned.1.call-start = ((), (), s32[]{:S(2)}) async-start(), calls=%async_computation.11 | async-start | bytes 3096576
  460.7 23.6 %collective-permute-start.45 = (f32[200,768]{1,0:T(8,128)}, f32[200,768]{1,0:T(8,128)}, u32[]{:S(2)}, u32[]{:S(2)}) collective-permute-start(f32[200,768]{1,0:T(8,128)} %slice.609), channel_id=1, source_target_pairs={{0,1},{1,0},{2,3},{3,2},{4,5},{5,4},{6,7},{7,6},{8,9},{9,8},{10,11... | collective-permute-start | bytes 1843208 | tf_op jit(solution)/shard_map/ppermute | solution.py:135
  475.7 226.6 %reduce-scatter.15.cloned.1.call-start = ((), (), s32[]{:S(2)}) async-start(), calls=%async_computation.9 | async-start | bytes 3096576
  480.4 7.5 %collective-permute-start.42 = (f32[200,768]{1,0:T(8,128)}, f32[200,768]{1,0:T(8,128)S(1)}, u32[]{:S(2)}, u32[]{:S(2)}) collective-permute-start(f32[200,768]{1,0:T(8,128)} %slice.605), channel_id=1, source_target_pairs={{0,1},{1,0},{2,3},{3,2},{4,5},{5,4},{6,7},{7,6},{8,9},{9,8},{10,11... | collective-permute-start | bytes 1843208 | tf_op jit(solution)/shard_map/ppermute | solution.py:135
  486.4 17.0 %collective-permute-start.46 = (f32[200,768]{1,0:T(8,128)}, f32[200,768]{1,0:T(8,128)}, u32[]{:S(2)}, u32[]{:S(2)}) collective-permute-start(f32[200,768]{1,0:T(8,128)} %slice_add_fusion), channel_id=1, source_target_pairs={{0,2},{2,0},{1,3},{3,1},{4,6},{6,4},{5,7},{7,5},{8,10},{10,8},{9,1... | collective-permute-start | bytes 1843208 | tf_op jit(solution)/shard_map/ppermute | solution.py:136
  488.8 27.3 %collective-permute-start.43 = (f32[200,768]{1,0:T(8,128)}, f32[200,768]{1,0:T(8,128)}, u32[]{:S(2)}, u32[]{:S(2)}) collective-permute-start(f32[200,768]{1,0:T(8,128)} %slice_add_fusion.1), channel_id=1, source_target_pairs={{0,2},{2,0},{1,3},{3,1},{4,6},{6,4},{5,7},{7,5},{8,10},{10,8},{9,1... | collective-permute-start | bytes 1843208 | tf_op jit(solution)/shard_map/ppermute | solution.py:136
  504.8 19.1 %collective-permute-start.47 = (f32[200,768]{1,0:T(8,128)S(1)}, f32[200,768]{1,0:T(8,128)}, u32[]{:S(2)}, u32[]{:S(2)}) collective-permute-start(f32[200,768]{1,0:T(8,128)S(1)} %get-tuple-element.131), channel_id=1, source_target_pairs={{0,1},{1,0},{2,3},{3,2},{4,5},{5,4},{6,7},{7,6},{8,9},{9,8},{10,11... | collective-permute-start | bytes 1843208 | tf_op jit(solution)/shard_map/ppermute | solution.py:137
  517.4 7.7 %collective-permute-start.44 = (f32[200,768]{1,0:T(8,128)S(1)}, f32[200,768]{1,0:T(8,128)}, u32[]{:S(2)}, u32[]{:S(2)}) collective-permute-start(f32[200,768]{1,0:T(8,128)S(1)} %get-tuple-element.129), channel_id=1, source_target_pairs={{0,1},{1,0},{2,3},{3,2},{4,5},{5,4},{6,7},{7,6},{8,9},{9,8},{10,11... | collective-permute-start | bytes 1843208 | tf_op jit(solution)/shard_map/ppermute | solution.py:137
  (112 other events, 576.0 us)
Sparse Core Ops, SparseCore 0:
  15.0 45.1 all-gather.4
  63.0 50.6 all-gather.6
  116.4 40.8 all-gather.8
  159.9 50.5 all-gather.10
  361.8 94.1 reduce-scatter.16
  459.4 95.0 reduce-scatter.12
  558.0 70.5 reduce-scatter.18
  632.2 70.1 reduce-scatter.14
